TPU v7x, 32 devices: a whole 2x2x4 slice. The times are simulated.
32 devices in a mesh: seq: 4 (over y, core), fsdp: 8 (over z, x).
Axes of the slice: x: 2, y: 2, z: 4, core: 2. Of those that a mesh axis runs over, the one named last changes fastest.
Arguments:
- frames_in: bfloat16 [8, 1024, 768], P('fsdp', 'seq'), may hold values from -6 to 6
- norm1_gain: bfloat16 [2, 768], P(None, 'fsdp'), may hold values from 0.25 to 1.75
- norm1_bias: bfloat16 [2, 768], P(None, 'fsdp'), may hold values from -3 to 3
- qkv_weight: bfloat16 [2, 768, 2304], P(None, 'fsdp'), may hold values from -0.3125 to 0.3125
- qv_bias: bfloat16 [2, 2, 768], P(None, None, 'fsdp'), may hold values from -0.59765625 to 0.59765625
- out_weight: bfloat16 [2, 768, 768], P(None, 'fsdp'), may hold values from -0.21875 to 0.21875
- out_bias: bfloat16 [2, 768], P(None, 'fsdp'), may hold values from -3 to 3
- norm2_gain: bfloat16 [2, 768], P(None, 'fsdp'), may hold values from 0.25 to 1.75
- norm2_bias: bfloat16 [2, 768], P(None, 'fsdp'), may hold values from -3 to 3
- fc1_weight: bfloat16 [2, 768, 3072], P(None, 'fsdp'), may hold values from -0.21875 to 0.21875
- fc1_bias: bfloat16 [2, 3072], P(None, 'fsdp'), may hold values from -3 to 3
- fc2_weight: bfloat16 [2, 3072, 768], P(None, 'fsdp'), may hold values from -0.109375 to 0.109375
- fc2_bias: bfloat16 [2, 768], P(None, 'fsdp'), may hold values from -3 to 3
- out_cotangent: bfloat16 [8, 1024, 768], P('fsdp', 'seq'), may hold values from -6 to 6
Outputs:
- frames_out: bfloat16 [8, 1024, 768], P('fsdp', 'seq')
- frames_grad: float32 [8, 1024, 768], P('fsdp', 'seq')
- norm1_gain_grad: float32 [2, 768], P(None, 'fsdp')
- norm1_bias_grad: float32 [2, 768], P(None, 'fsdp')
- qkv_weight_grad: float32 [2, 768, 2304], P(None, 'fsdp')
- qv_bias_grad: float32 [2, 2, 768], P(None, None, 'fsdp')
- out_weight_grad: float32 [2, 768, 768], P(None, 'fsdp')
- out_bias_grad: float32 [2, 768], P(None, 'fsdp')
- norm2_gain_grad: float32 [2, 768], P(None, 'fsdp')
- norm2_bias_grad: float32 [2, 768], P(None, 'fsdp')
- fc1_weight_grad: float32 [2, 768, 3072], P(None, 'fsdp')
- fc1_bias_grad: float32 [2, 3072], P(None, 'fsdp')
- fc2_weight_grad: float32 [2, 3072, 768], P(None, 'fsdp')
- fc2_bias_grad: float32 [2, 768], P(None, 'fsdp')
All inputs are finite; a program needn't handle non-finite values.
Results may differ from a plain program's by a relative error of at most 0.023.
Values may be sent and summed in bfloat16 or wider, within the bound.
A program may use at most 192 MiB of HBM per device.

v0:
```python
from functools import partial
import math

import jax
import jax.numpy as jnp
from jax import lax
from jax.sharding import PartitionSpec as P

D = 768
HEADS = 12
HEAD_DIM = 64


EPSILON = 1e-05


def norm_rows(values, gain, shift):
    center = jnp.mean(values, axis=-1, keepdims=True)
    centred = values - center
    spread = jnp.mean(centred * centred, axis=-1, keepdims=True)
    return centred * lax.rsqrt(spread + EPSILON) * gain + shift


def qkv_shift(pair_bias):
    query_part = pair_bias[0].reshape(HEADS, 1, HEAD_DIM)
    value_part = pair_bias[1].reshape(HEADS, 1, HEAD_DIM)
    joined = jnp.concatenate([query_part, jnp.zeros_like(query_part), value_part], axis=1)
    return joined.reshape(3 * D)


def forward_weights(shards, layer_index):
    (
        gain_one,
        shift_one,
        w_qkv,
        qv_pair,
        w_out,
        out_shift,
        gain_two,
        shift_two,
        w_up,
        up_shift,
        w_down,
        down_shift,
    ) = tuple((piece[layer_index] for piece in shards))
    return (
        lax.all_gather(gain_one, "fsdp", axis=0, tiled=True),
        lax.all_gather(shift_one, "fsdp", axis=0, tiled=True),
        lax.all_gather(w_qkv, "fsdp", axis=0, tiled=True),
        lax.all_gather(qv_pair, "fsdp", axis=1, tiled=True),
        lax.all_gather(w_out, "fsdp", axis=0, tiled=True),
        lax.all_gather(out_shift, "fsdp", axis=0, tiled=True),
        lax.all_gather(gain_two, "fsdp", axis=0, tiled=True),
        lax.all_gather(shift_two, "fsdp", axis=0, tiled=True),
        lax.all_gather(w_up, "fsdp", axis=0, tiled=True),
        lax.all_gather(up_shift, "fsdp", axis=0, tiled=True),
        lax.all_gather(w_down, "fsdp", axis=0, tiled=True),
        lax.all_gather(down_shift, "fsdp", axis=0, tiled=True),
    )


def backward_weights(shards, layer_index):
    (
        gain_one,
        shift_one,
        w_qkv,
        qv_pair,
        w_out,
        out_shift,
        gain_two,
        shift_two,
        w_up,
        up_shift,
        w_down,
        down_shift,
    ) = tuple((piece[layer_index] for piece in shards))
    return (
        lax.all_gather(gain_one, "fsdp", axis=0, tiled=True),
        lax.all_gather(shift_one, "fsdp", axis=0, tiled=True),
        lax.all_gather(w_qkv, "fsdp", axis=0, tiled=True),
        lax.all_gather(qv_pair, "fsdp", axis=1, tiled=True),
        lax.all_gather(w_out, "fsdp", axis=0, tiled=True),
        lax.all_gather(out_shift, "fsdp", axis=0, tiled=True),
        lax.all_gather(gain_two, "fsdp", axis=0, tiled=True),
        lax.all_gather(shift_two, "fsdp", axis=0, tiled=True),
        lax.all_gather(w_up, "fsdp", axis=0, tiled=True),
        lax.all_gather(up_shift, "fsdp", axis=0, tiled=True),
        lax.all_gather(w_down, "fsdp", axis=0, tiled=True),
        lax.all_gather(down_shift, "fsdp", axis=0, tiled=True),
    )


def reduce_partials(partials):
    (
        gain_one,
        shift_one,
        w_qkv,
        qv_pair,
        w_out,
        out_shift,
        gain_two,
        shift_two,
        w_up,
        up_shift,
        w_down,
        down_shift,
    ) = partials
    owned = (
        lax.psum_scatter(gain_one, "fsdp", scatter_dimension=0, tiled=True),
        lax.psum_scatter(shift_one, "fsdp", scatter_dimension=0, tiled=True),
        lax.psum_scatter(w_qkv, "fsdp", scatter_dimension=0, tiled=True),
        lax.psum_scatter(qv_pair, "fsdp", scatter_dimension=1, tiled=True),
        lax.psum_scatter(w_out, "fsdp", scatter_dimension=0, tiled=True),
        lax.psum_scatter(out_shift, "fsdp", scatter_dimension=0, tiled=True),
        lax.psum_scatter(gain_two, "fsdp", scatter_dimension=0, tiled=True),
        lax.psum_scatter(shift_two, "fsdp", scatter_dimension=0, tiled=True),
        lax.psum_scatter(w_up, "fsdp", scatter_dimension=0, tiled=True),
        lax.psum_scatter(up_shift, "fsdp", scatter_dimension=0, tiled=True),
        lax.psum_scatter(w_down, "fsdp", scatter_dimension=0, tiled=True),
        lax.psum_scatter(down_shift, "fsdp", scatter_dimension=0, tiled=True),
    )
    member_shapes = [member.shape for member in owned]
    flat_all = jnp.concatenate([member.reshape(-1) for member in owned])
    own_quarter = lax.psum_scatter(
        flat_all.astype(jnp.bfloat16), "seq", scatter_dimension=0, tiled=True
    ).astype(jnp.float32)
    whole = lax.all_gather(own_quarter.astype(jnp.bfloat16), "seq", axis=0, tiled=True).astype(
        own_quarter.dtype
    )
    results = []
    offset = 0
    for member_shape in member_shapes:
        member_size = math.prod(member_shape)
        results.append(whole[offset : offset + member_size].reshape(member_shape))
        offset = offset + member_size
    return tuple(results)


def attend_forward(packed):
    frames = packed.shape[0]
    local_heads = packed.shape[1] // (3 * HEAD_DIM)
    parts = packed.reshape(frames, local_heads, 3, HEAD_DIM)
    scores = jnp.einsum(
        "qhd,khd->hqk", parts[:, :, 0], parts[:, :, 1], preferred_element_type=jnp.float32
    ) * HEAD_DIM ** (-0.5)
    peak_score = jnp.max(scores, axis=-1, keepdims=True)
    expanded = jnp.exp(scores - peak_score)
    totals = jnp.sum(expanded, axis=-1, keepdims=True)
    weights = (expanded / totals).astype(jnp.bfloat16)
    mixed = jnp.einsum("hqk,khd->qhd", weights, parts[:, :, 2], preferred_element_type=jnp.float32)
    return (
        mixed.reshape(frames, local_heads * HEAD_DIM).astype(jnp.bfloat16),
        (peak_score + jnp.log(totals))[..., 0],
    )


def attend_backward(inputs):
    packed, log_total, incoming = inputs
    frames = packed.shape[0]
    local_heads = packed.shape[1] // (3 * HEAD_DIM)
    parts = packed.reshape(frames, local_heads, 3, HEAD_DIM)
    queries = parts[:, :, 0]
    keys_local = parts[:, :, 1]
    values_local = parts[:, :, 2]
    scale = HEAD_DIM ** (-0.5)
    scores = (
        jnp.einsum("qhd,khd->hqk", queries, keys_local, preferred_element_type=jnp.float32) * scale
    )
    probs = jnp.exp(scores - log_total[..., None])
    incoming_heads = incoming.reshape(frames, local_heads, HEAD_DIM)
    grad_probs = jnp.einsum(
        "qhd,khd->hqk", incoming_heads, values_local, preferred_element_type=jnp.float32
    )
    grad_values = jnp.einsum(
        "hqk,qhd->khd",
        probs.astype(jnp.bfloat16),
        incoming_heads,
        preferred_element_type=jnp.float32,
    )
    grad_scores = (
        probs * (grad_probs - jnp.sum(probs * grad_probs, axis=-1, keepdims=True))
    ).astype(jnp.bfloat16)
    grad_queries = (
        jnp.einsum("hqk,khd->qhd", grad_scores, keys_local, preferred_element_type=jnp.float32)
        * scale
    )
    grad_keys = (
        jnp.einsum("hqk,qhd->khd", grad_scores, queries, preferred_element_type=jnp.float32) * scale
    )
    stacked = jnp.stack([grad_queries, grad_keys, grad_values], axis=2)
    return stacked.reshape(frames, local_heads * 3 * HEAD_DIM).astype(jnp.bfloat16)


def layer_forward(stream, weights):
    (
        gain_one,
        shift_one,
        w_qkv,
        qv_pair,
        w_out,
        out_shift,
        gain_two,
        shift_two,
        w_up,
        up_shift,
        w_down,
        down_shift,
    ) = weights
    normed_one = norm_rows(
        stream, gain_one.astype(jnp.float32), shift_one.astype(jnp.float32)
    ).astype(jnp.bfloat16)
    projected = (
        jnp.einsum("cfi,io->cfo", normed_one, w_qkv, preferred_element_type=jnp.float32)
        + qkv_shift(qv_pair.astype(jnp.float32))
    ).astype(jnp.bfloat16)
    heads = lax.all_to_all(projected, "seq", split_axis=2, concat_axis=1, tiled=True)
    mixed_heads, log_total = lax.map(attend_forward, heads)
    mixed = lax.all_to_all(mixed_heads, "seq", split_axis=1, concat_axis=2, tiled=True)
    attended = stream + (
        jnp.einsum("cfi,io->cfo", mixed, w_out, preferred_element_type=jnp.float32)
        + out_shift.astype(jnp.float32)
    )
    normed_two = norm_rows(
        attended, gain_two.astype(jnp.float32), shift_two.astype(jnp.float32)
    ).astype(jnp.bfloat16)
    hidden = jnp.einsum(
        "cfi,io->cfo", normed_two, w_up, preferred_element_type=jnp.float32
    ) + up_shift.astype(jnp.float32)
    activated = jax.nn.gelu(hidden, approximate=False).astype(jnp.bfloat16)
    result = attended + (
        jnp.einsum("cfi,io->cfo", activated, w_down, preferred_element_type=jnp.float32)
        + down_shift.astype(jnp.float32)
    )
    return ((stream, normed_one, heads, log_total, mixed, attended, normed_two, hidden), result)


def layer_backward(upstream, weights, state):
    (
        gain_one,
        shift_one,
        w_qkv,
        qv_pair,
        w_out,
        out_shift,
        gain_two,
        shift_two,
        w_up,
        up_shift,
        w_down,
        down_shift,
    ) = weights
    stream, normed_one, heads, log_total, mixed, attended, normed_two, hidden = state
    grad_down = upstream.astype(jnp.bfloat16)
    activated = jax.nn.gelu(hidden, approximate=False).astype(jnp.bfloat16)
    down_shift_grad = jnp.sum(grad_down.astype(jnp.float32), axis=(0, 1))
    w_down_grad = jnp.einsum(
        "cfi,cfo->io", activated, grad_down, preferred_element_type=jnp.float32
    )
    grad_active = jnp.einsum("cfo,io->cfi", grad_down, w_down, preferred_element_type=jnp.float32)
    gelu_pull = jax.vjp(partial(jax.nn.gelu, approximate=False), hidden)[1]
    grad_hidden = gelu_pull(grad_active)[0].astype(jnp.bfloat16)
    up_shift_grad = jnp.sum(grad_hidden.astype(jnp.float32), axis=(0, 1))
    w_up_grad = jnp.einsum(
        "cfi,cfo->io", normed_two, grad_hidden, preferred_element_type=jnp.float32
    )
    grad_normed_two = jnp.einsum(
        "cfo,io->cfi", grad_hidden, w_up, preferred_element_type=jnp.float32
    )
    normed_again, pull_two = jax.vjp(
        norm_rows, attended, gain_two.astype(jnp.float32), shift_two.astype(jnp.float32)
    )
    grad_attended, gain_two_grad, shift_two_grad = pull_two(grad_normed_two)
    grad_attended = grad_attended + upstream
    grad_out = grad_attended.astype(jnp.bfloat16)
    out_shift_grad = jnp.sum(grad_out.astype(jnp.float32), axis=(0, 1))
    w_out_grad = jnp.einsum("cfi,cfo->io", mixed, grad_out, preferred_element_type=jnp.float32)
    grad_mixed = jnp.einsum(
        "cfo,io->cfi", grad_out, w_out, preferred_element_type=jnp.float32
    ).astype(jnp.bfloat16)
    grad_heads = lax.all_to_all(grad_mixed, "seq", split_axis=2, concat_axis=1, tiled=True)
    grad_packed = lax.map(attend_backward, (heads, log_total, grad_heads))
    grad_projected = lax.all_to_all(grad_packed, "seq", split_axis=1, concat_axis=2, tiled=True)
    summed = jnp.sum(grad_projected.astype(jnp.float32), axis=(0, 1)).reshape(HEADS, 3, HEAD_DIM)
    qv_pair_grad = jnp.stack([summed[:, 0].reshape(D), summed[:, 2].reshape(D)])
    w_qkv_grad = jnp.einsum(
        "cfi,cfo->io", normed_one, grad_projected, preferred_element_type=jnp.float32
    )
    grad_normed_one = jnp.einsum(
        "cfo,io->cfi", grad_projected, w_qkv, preferred_element_type=jnp.float32
    )
    normed_first, pull_one = jax.vjp(
        norm_rows, stream, gain_one.astype(jnp.float32), shift_one.astype(jnp.float32)
    )
    grad_stream, gain_one_grad, shift_one_grad = pull_one(grad_normed_one)
    grad_stream = grad_stream + grad_attended
    partials = (
        gain_one_grad,
        shift_one_grad,
        w_qkv_grad,
        qv_pair_grad,
        w_out_grad,
        out_shift_grad,
        gain_two_grad,
        shift_two_grad,
        w_up_grad,
        up_shift_grad,
        w_down_grad,
        down_shift_grad,
    )
    return (grad_stream, partials)


def local(
    frames_in,
    norm1_gain,
    norm1_bias,
    qkv_weight,
    qv_bias,
    out_weight,
    out_bias,
    norm2_gain,
    norm2_bias,
    fc1_weight,
    fc1_bias,
    fc2_weight,
    fc2_bias,
    out_cotangent,
):
    shards = (
        norm1_gain,
        norm1_bias,
        qkv_weight,
        qv_bias,
        out_weight,
        out_bias,
        norm2_gain,
        norm2_bias,
        fc1_weight,
        fc1_bias,
        fc2_weight,
        fc2_bias,
    )
    layer_count = qkv_weight.shape[0]
    stream = frames_in.astype(jnp.float32)
    saved = []
    fetched = []
    for layer_index in range(layer_count):
        weights = forward_weights(shards, layer_index)
        fetched.append(weights)
        kept_state, stream = layer_forward(stream, weights)
        saved.append(kept_state)
    frames_out = stream.astype(jnp.bfloat16)
    upstream = out_cotangent.astype(jnp.float32)
    reduced = [None] * layer_count
    for layer_index in reversed(range(layer_count)):
        weights = backward_weights(shards, layer_index)
        upstream, partials = layer_backward(upstream, weights, saved[layer_index])
        reduced[layer_index] = reduce_partials(partials)
    stacked = tuple(
        (
            jnp.stack([reduced[level][member] for level in range(layer_count)])
            for member in range(12)
        )
    )
    return (frames_out, upstream) + stacked


def solution(mesh):
    in_specs = (
        P("fsdp", "seq", None),
        P(None, "fsdp"),
        P(None, "fsdp"),
        P(None, "fsdp", None),
        P(None, None, "fsdp"),
        P(None, "fsdp", None),
        P(None, "fsdp"),
        P(None, "fsdp"),
        P(None, "fsdp"),
        P(None, "fsdp", None),
        P(None, "fsdp"),
        P(None, "fsdp", None),
        P(None, "fsdp"),
        P("fsdp", "seq", None),
    )
    out_specs = (
        P("fsdp", "seq", None),
        P("fsdp", "seq", None),
        P(None, "fsdp"),
        P(None, "fsdp"),
        P(None, "fsdp", None),
        P(None, None, "fsdp"),
        P(None, "fsdp", None),
        P(None, "fsdp"),
        P(None, "fsdp"),
        P(None, "fsdp"),
        P(None, "fsdp", None),
        P(None, "fsdp"),
        P(None, "fsdp", None),
        P(None, "fsdp"),
    )
    return jax.shard_map(local, mesh=mesh, in_specs=in_specs, out_specs=out_specs, check_vma=False)
```

profile of v0, /device:TPU:0, one launch (start us, length us, event | category | flops | bytes accessed | tf_op | source)
XLA Modules:
  0.0 2234.5 jit_solution(13550334198232716625)
XLA Ops:
  19.8 40.2 %all-reduce.31 = (bf16[768]{0:T(1024)(128)(2,1)S(1)}, bf16[768]{0:T(1024)(128)(2,1)S(1)}, bf16[768]{0:T(1024)(128)(2,1)S(1)}, bf16[768]{0:T(1024)(128)(2,1)S(1)}...) all-reduce(bf16[768]{0:T(1024)(128)(2,1)S(1)} %dynamic-update-slice, ...), channel_id=3, replica_groups=mesh['seq'=4,'fsdp'=8] {'fsdp'}, use_global_device_ids=true, to_apply=%add.1 | all-reduce | flops 9216 | bytes 36864
  60.3 31.7 %all-gather.3 = bf16[1,2,768]{1,0,2:T(2,128)(2,1)S(1)} all-gather(bf16[1,2,96]{1,0,2:T(2,128)(2,1)S(1)} %copy.234), channel_id=5, replica_groups=mesh['seq'=4,'fsdp'=8] {'fsdp'}, dimensions={2}, use_global_device_ids=true | all-gather | bytes 3456 | tf_op jit(solution)/shard_map/all_gather | solution.py:50
  97.1 31.7 %all-gather.15 = bf16[1,2,768]{1,0,2:T(2,128)(2,1)S(1)} all-gather(bf16[1,2,96]{1,0,2:T(2,128)(2,1)S(1)} %copy.238), channel_id=17, replica_groups=mesh['seq'=4,'fsdp'=8] {'fsdp'}, dimensions={2}, use_global_device_ids=true | all-gather | bytes 3456 | tf_op jit(solution)/shard_map/all_gather | solution.py:50
  205.1 26.5 %all-gather.9 = bf16[1,3072]{1,0:T(2,128)(2,1)S(1)} all-gather(bf16[1,384]{1,0:T(2,128)(2,1)S(1)} %get-tuple-element.156), channel_id=11, replica_groups=mesh['seq'=4,'fsdp'=8] {'fsdp'}, dimensions={1}, use_global_device_ids=true | all-gather | bytes 6912 | tf_op jit(solution)/shard_map/all_gather | solution.py:56
  247.2 42.4 %all-gather.39.cloned.1.call-done = bf16[1,3072,768]{2,1,0:T(8,128)(2,1)} async-done(((bf16[1,384,768]{2,1,0:T(8,128)(2,1)}), bf16[1,3072,768]{2,1,0:T(8,128)(2,1)}) %all-gather.39.cloned.1.call-update) | async-done | bytes 4718608 | tf_op jit(solution)/shard_map/all_gather | solution.py:57
  293.7 61.3 %all-gather.41.cloned.1.call-done = bf16[1,768,2304]{2,1,0:T(8,128)(2,1)} async-done(((bf16[1,96,2304]{2,1,0:T(8,128)(2,1)}), bf16[1,768,2304]{2,1,0:T(8,128)(2,1)}) %all-gather.41.cloned.1.call-update) | async-done | bytes 3538960 | tf_op jit(solution)/shard_map/all_gather | solution.py:49
  376.9 19.5 all_to_all.121
  424.0 26.4 %all-gather.21 = bf16[1,3072]{1,0:T(2,128)(2,1)S(1)} all-gather(bf16[1,384]{1,0:T(2,128)(2,1)S(1)} %get-tuple-element.155), channel_id=23, replica_groups=mesh['seq'=4,'fsdp'=8] {'fsdp'}, dimensions={1}, use_global_device_ids=true | all-gather | bytes 6912 | tf_op jit(solution)/shard_map/all_gather | solution.py:56
  455.0 23.1 %all-gather.45.cloned.1.call-done = bf16[1,768,3072]{2,1,0:T(8,128)(2,1)} async-done(((bf16[1,96,3072]{2,1,0:T(8,128)(2,1)}), bf16[1,768,3072]{2,1,0:T(8,128)(2,1)}) %all-gather.45.cloned.1.call-update) | async-done | bytes 4718608 | tf_op jit(solution)/shard_map/all_gather | solution.py:55
  489.8 69.2 %all-gather.47.cloned.1.call-done = bf16[1,3072,768]{2,1,0:T(8,128)(2,1)} async-done(((bf16[1,384,768]{2,1,0:T(8,128)(2,1)}), bf16[1,3072,768]{2,1,0:T(8,128)(2,1)}) %all-gather.47.cloned.1.call-update) | async-done | bytes 4718608 | tf_op jit(solution)/shard_map/all_gather | solution.py:57
  646.1 20.4 all_to_all.122
  858.5 35.7 %all-reduce.30 = (bf16[768]{0:T(1024)(128)(2,1)S(1)}, bf16[768]{0:T(1024)(128)(2,1)S(1)}, bf16[768]{0:T(1024)(128)(2,1)S(1)}, bf16[768]{0:T(1024)(128)(2,1)S(1)}...) all-reduce(f32[768]{0:T(1024)S(1)} %copy-done.97, ...), channel_id=39, replica_groups=mesh['seq'=4,'fsdp'=8] {'fsdp'}, use_global_device_ids=true, to_apply=%region_44.45.clone | all-reduce | flops 15360 | bytes 92160
  901.4 71.2 %reduce-scatter.25.cloned.1.call-done = f32[96,768]{1,0:T(8,128)} async-done(((f32[768,768]{1,0:T(8,128)}), f32[96,768]{1,0:T(8,128)}) %reduce-scatter.25.cloned.1.call-update) | async-done | bytes 294928 | tf_op jit(solution)/shard_map/reduce_scatter | solution.py:113
  973.7 70.8 %reduce-scatter.17.cloned.1.call-done = f32[96,768]{1,0:T(8,128)} async-done(((f32[768,768]{1,0:T(8,128)}), f32[96,768]{1,0:T(8,128)}) %reduce-scatter.17.cloned.1.call-update) | async-done | bytes 294928 | tf_op jit(solution)/shard_map/reduce_scatter | solution.py:113
  1045.6 130.6 %reduce-scatter.23.cloned.1.call-done = f32[96,2304]{1,0:T(8,128)} async-done(((f32[768,2304]{1,0:T(8,128)}), f32[96,2304]{1,0:T(8,128)}) %reduce-scatter.23.cloned.1.call-update) | async-done | bytes 884752 | tf_op jit(solution)/shard_map/reduce_scatter | solution.py:111
  1180.6 127.8 %reduce-scatter.15.cloned.1.call-done = f32[96,2304]{1,0:T(8,128)} async-done(((f32[768,2304]{1,0:T(8,128)}), f32[96,2304]{1,0:T(8,128)}) %reduce-scatter.15.cloned.1.call-update) | async-done | bytes 884752 | tf_op jit(solution)/shard_map/reduce_scatter | solution.py:111
  1312.7 161.6 %reduce-scatter.27.cloned.1.call-done = f32[96,3072]{1,0:T(8,128)} async-done(((f32[768,3072]{1,0:T(8,128)}), f32[96,3072]{1,0:T(8,128)}) %reduce-scatter.27.cloned.1.call-update) | async-done | bytes 1179664 | tf_op jit(solution)/shard_map/reduce_scatter | solution.py:117
  1476.5 163.7 %reduce-scatter.29.cloned.1.call-done = f32[384,768]{1,0:T(8,128)} async-done(((f32[3072,768]{1,0:T(8,128)}), f32[384,768]{1,0:T(8,128)}) %reduce-scatter.29.cloned.1.call-update) | async-done | bytes 1179664 | tf_op jit(solution)/shard_map/reduce_scatter | solution.py:119
  1644.7 35.5 %concatenate.17 = bf16[885888]{0:T(1024)(128)(2,1)} concatenate(bf16[96]{0:T(256)(128)(2,1)S(1)} %dynamic-slice.67, bf16[96]{0:T(256)(128)(2,1)S(1)} %dynamic-slice.66, bf16[221184]{0:T(1024)(128)(2,1)} %reshape.788, bf16[192]{0:T(256)(128)(2,1)S(1)} %reshape.790, bf16[73728]{0:T(1024)(128)(2,1)S(1)} %reshape.791, bf16[96]{0:T(256)(128)(2,1)S(1)} %dynamic-slice.65, ...), dimensions={0} | concatenate | bytes 3543552 | tf_op jit(solution)/shard_map/concatenate | solution.py:123
  1680.2 125.9 %reduce-scatter.19.cloned.1.call-done = f32[96,3072]{1,0:T(8,128)} async-done(((f32[768,3072]{1,0:T(8,128)}), f32[96,3072]{1,0:T(8,128)}) %reduce-scatter.19.cloned.1.call-update) | async-done | bytes 1179664 | tf_op jit(solution)/shard_map/reduce_scatter | solution.py:117
  1808.4 163.6 %reduce-scatter.21.cloned.1.call-done = f32[384,768]{1,0:T(8,128)} async-done(((f32[3072,768]{1,0:T(8,128)}), f32[384,768]{1,0:T(8,128)}) %reduce-scatter.21.cloned.1.call-update) | async-done | bytes 1179664 | tf_op jit(solution)/shard_map/reduce_scatter | solution.py:119
  1976.5 35.4 %concatenate.16 = bf16[885888]{0:T(1024)(128)(2,1)} concatenate(bf16[96]{0:T(256)(128)(2,1)S(1)} %dynamic-slice.73, bf16[96]{0:T(256)(128)(2,1)S(1)} %dynamic-slice.72, bf16[221184]{0:T(1024)(128)(2,1)} %reshape.782, bf16[192]{0:T(256)(128)(2,1)S(1)} %reshape.784, bf16[73728]{0:T(1024)(128)(2,1)S(1)} %reshape.785, bf16[96]{0:T(256)(128)(2,1)S(1)} %dynamic-slice.71, ...), dimensions={0} | concatenate | bytes 3543552 | tf_op jit(solution)/shard_map/concatenate | solution.py:123
  2013.2 73.4 %all-reduce.39.cloned.1.call-done = (bf16[885888]{0:T(1024)(128)(2,1)}, bf16[885888]{0:T(1024)(128)(2,1)}) async-done(((bf16[885888]{0:T(1024)(128)(2,1)}, bf16[885888]{0:T(1024)(128)(2,1)}), (bf16[885888]{0:T(1024)(128)(2,1)}, bf16[885888]{0:T(1024)(128)(2,1)})) %all-reduce.39.cloned.1.call-update) | async-done | bytes 3543568
  2115.2 69.3 %all-reduce.37.cloned.1.call-done = (bf16[885888]{0:T(1024)(128)(2,1)}, bf16[885888]{0:T(1024)(128)(2,1)}) async-done(((bf16[885888]{0:T(1024)(128)(2,1)}, bf16[885888]{0:T(1024)(128)(2,1)}), (bf16[885888]{0:T(1024)(128)(2,1)}, bf16[885888]{0:T(1024)(128)(2,1)})) %all-reduce.37.cloned.1.call-update) | async-done | bytes 3543568
  (618 shorter events, 557.7 us)
Async XLA Ops:
  7.2 127.6 %all-gather.33.cloned.1.call-start = ((), (), s32[]{:S(2)}) async-start(), calls=%async_computation.26 | async-start | bytes 3981312 | tf_op jit(solution)/shard_map/all_gather | solution.py:49
  9.5 223.9 %all-gather.35.cloned.1.call-start = ((), (), s32[]{:S(2)}) async-start(), calls=%async_computation.27 | async-start | bytes 1327104 | tf_op jit(solution)/shard_map/all_gather | solution.py:51
  11.4 224.3 %all-gather.37.cloned.1.call-start = ((), (), s32[]{:S(2)}) async-start(), calls=%async_computation.28 | async-start | bytes 5308416 | tf_op jit(solution)/shard_map/all_gather | solution.py:55
  12.6 277.0 %all-gather.39.cloned.1.call-start = ((), (), s32[]{:S(2)}) async-start(), calls=%async_computation.29 | async-start | bytes 5308416 | tf_op jit(solution)/shard_map/all_gather | solution.py:57
  13.8 341.2 %all-gather.41.cloned.1.call-start = ((), (), s32[]{:S(2)}) async-start(), calls=%async_computation.30 | async-start | bytes 3981312 | tf_op jit(solution)/shard_map/all_gather | solution.py:49
  14.4 438.4 %all-gather.43.cloned.1.call-start = ((), (), s32[]{:S(2)}) async-start(), calls=%async_computation.31 | async-start | bytes 1327104 | tf_op jit(solution)/shard_map/all_gather | solution.py:51
  15.0 463.2 %all-gather.45.cloned.1.call-start = ((), (), s32[]{:S(2)}) async-start(), calls=%async_computation.32 | async-start | bytes 5308416 | tf_op jit(solution)/shard_map/all_gather | solution.py:55
  200.7 31.0 %all-to-all-start.1 = ((bf16[4,2,24576]{2,1,0:T(2,128)(2,1)}), bf16[4,2,24576]{2,1,0:T(2,128)(2,1)S(1)}, u32[]{:S(2)}, u32[]{:S(2)}) async-start(bf16[4,2,24576]{2,1,0:T(2,128)(2,1)} %reshape.969), calls=%async_computation.1 | async-start | bytes 786432 | tf_op jit(solution)/shard_map/all_to_all | solution.py:218
  204.2 354.8 %all-gather.47.cloned.1.call-start = ((), (), s32[]{:S(2)}) async-start(), calls=%async_computation.33 | async-start | bytes 5308416 | tf_op jit(solution)/shard_map/all_gather | solution.py:57
  420.5 30.6 %all-to-all-start.3 = ((bf16[4,2,24576]{2,1,0:T(2,128)(2,1)}), bf16[4,2,24576]{2,1,0:T(2,128)(2,1)S(1)}, u32[]{:S(2)}, u32[]{:S(2)}) async-start(bf16[4,2,24576]{2,1,0:T(2,128)(2,1)} %reshape.973), calls=%async_computation.3 | async-start | bytes 786432 | tf_op jit(solution)/shard_map/all_to_all | solution.py:218
  582.2 11.6 all-to-all-start.4
  767.2 20.2 all-to-all-start.7
  771.5 81.7 %reduce-scatter.33.cloned.1.call-start = ((), (), s32[]{:S(2)}) async-start(), calls=%async_computation.35 | async-start | bytes 442368
  774.9 125.5 %reduce-scatter.31.cloned.1.call-start = ((), (), s32[]{:S(2)}) async-start(), calls=%async_computation.34 | async-start | bytes 442368
  801.9 170.7 %reduce-scatter.25.cloned.1.call-start = ((), (), s32[]{:S(2)}) async-start(), calls=%async_computation.23 | async-start | bytes 2654208 | tf_op jit(solution)/shard_map/reduce_scatter | solution.py:113
  805.0 239.5 %reduce-scatter.17.cloned.1.call-start = ((), (), s32[]{:S(2)}) async-start(), calls=%async_computation.19 | async-start | bytes 2654208 | tf_op jit(solution)/shard_map/reduce_scatter | solution.py:113
  808.2 368.1 %reduce-scatter.23.cloned.1.call-start = ((), (), s32[]{:S(2)}) async-start(), calls=%async_computation.22 | async-start | bytes 7962624 | tf_op jit(solution)/shard_map/reduce_scatter | solution.py:111
  813.7 494.7 %reduce-scatter.15.cloned.1.call-start = ((), (), s32[]{:S(2)}) async-start(), calls=%async_computation.18 | async-start | bytes 7962624 | tf_op jit(solution)/shard_map/reduce_scatter | solution.py:111
  820.5 653.8 %reduce-scatter.27.cloned.1.call-start = ((), (), s32[]{:S(2)}) async-start(), calls=%async_computation.24 | async-start | bytes 10616832 | tf_op jit(solution)/shard_map/reduce_scatter | solution.py:117
  827.8 812.4 %reduce-scatter.29.cloned.1.call-start = ((), (), s32[]{:S(2)}) async-start(), calls=%async_computation.25 | async-start | bytes 10616832 | tf_op jit(solution)/shard_map/reduce_scatter | solution.py:119
  835.4 970.8 %reduce-scatter.19.cloned.1.call-start = ((), (), s32[]{:S(2)}) async-start(), calls=%async_computation.20 | async-start | bytes 10616832 | tf_op jit(solution)/shard_map/reduce_scatter | solution.py:117
  842.7 1129.3 %reduce-scatter.21.cloned.1.call-start = ((), (), s32[]{:S(2)}) async-start(), calls=%async_computation.21 | async-start | bytes 10616832 | tf_op jit(solution)/shard_map/reduce_scatter | solution.py:119
  849.3 1237.3 %all-reduce.39.cloned.1.call-start = ((), (), s32[]{:S(2)}) async-start(), calls=%async_computation.37 | async-start | bytes 7094272
  2012.0 172.5 %all-reduce.37.cloned.1.call-start = ((), (), s32[]{:S(2)}) async-start(), calls=%async_computation.36 | async-start | bytes 7094272
  (131 other events, 1963.7 us)
Sparse Core Ops, SparseCore 0:
  10.8 73.8 all-gather.32
  86.9 40.2 all-gather.34
  130.0 78.8 all-gather.36
  211.5 78.0 all-gather.38
  291.6 63.3 all-gather.40
  357.0 39.5 all-gather.42
  399.4 78.7 all-gather.44
  480.9 78.0 all-gather.46
  776.2 59.9 reduce-scatter.32
  839.9 60.5 reduce-scatter.30
  904.5 67.9 reduce-scatter.24
  976.5 67.9 reduce-scatter.16
  1048.2 128.0 reduce-scatter.22
  1180.3 128.0 reduce-scatter.14
  1311.8 162.3 reduce-scatter.26
  1477.7 162.4 reduce-scatter.28
  1643.7 162.3 reduce-scatter.18
  1809.6 162.4 reduce-scatter.20
  2012.1 74.5 all-reduce.38
  2109.0 75.4 all-reduce.36
where the time goes:
time: 2250 us; the launch traced here: 2230 us
  waiting for transfers between devices  1390 us (62%)
  local copies, waits for them, and re-layouts  271 us (12%)
  blocking collectives  251 us (11%)
  matrix products  160 us (7%)
  other arithmetic  124 us (6%)
    reduce_scatter x2, waiting for transfers between devices, reduce_partials(): lax.psum_scatter(w_down, 'fsdp', scatter_dimension=0, tiled=True)  327 us
    reduce_scatter x2, waiting for transfers between devices, reduce_partials(): lax.psum_scatter(w_up, 'fsdp', scatter_dimension=0, tiled=True)  287 us
    reduce_scatter x2, waiting for transfers between devices, reduce_partials(): lax.psum_scatter(w_qkv, 'fsdp', scatter_dimension=0, tiled=True)  258 us
    unnamed x24, waiting for transfers between devices  151 us
    reduce_scatter x2, waiting for transfers between devices, reduce_partials(): lax.psum_scatter(w_out, 'fsdp', scatter_dimension=0, tiled=True)  142 us
    all_gather x2, waiting for transfers between devices, forward_weights(): lax.all_gather(w_down, 'fsdp', axis=0, tiled=True)  112 us
    unnamed x342, local copies, waits for them, and re-layouts  94.3 us
    unnamed x2, blocking collectives  75.9 us
  transfers between devices with their start and end apart: 25, of which 18 were waited for; matrix products, arithmetic and copies ran while one was open for 12% of the time, Pallas kernels for 0%

commit v1 on v0

v1 whole, which is shorter than its diff:
```python
from functools import partial
import math

import jax
import jax.numpy as jnp
from jax import lax
from jax.sharding import PartitionSpec as P

D = 768
HEADS = 12
HEAD_DIM = 64


EPSILON = 1e-05


def norm_rows(values, gain, shift):
    center = jnp.mean(values, axis=-1, keepdims=True)
    centred = values - center
    spread = jnp.mean(centred * centred, axis=-1, keepdims=True)
    return centred * lax.rsqrt(spread + EPSILON) * gain + shift


def qkv_shift(pair_bias):
    query_part = pair_bias[0].reshape(HEADS, 1, HEAD_DIM)
    value_part = pair_bias[1].reshape(HEADS, 1, HEAD_DIM)
    joined = jnp.concatenate([query_part, jnp.zeros_like(query_part), value_part], axis=1)
    return joined.reshape(3 * D)


BF = jnp.bfloat16
F32 = jnp.float32


def seq_gather(block):
    return lax.all_gather(block, "seq", axis=1, tiled=True)


def seq_reduce(partial_sum):
    summed = lax.psum_scatter(partial_sum.astype(BF), "seq", scatter_dimension=1, tiled=True)
    return summed.astype(F32)


def dot_in(rows, matrix):
    return jnp.einsum("cfi,io->cfo", rows, matrix, preferred_element_type=F32)


def dot_back(rows, matrix):
    return jnp.einsum("cfo,io->cfi", rows, matrix, preferred_element_type=F32)


def dot_grad(left, right):
    return jnp.einsum("cfi,cfo->io", left, right, preferred_element_type=F32)


def take_part(array, axis, parts, index):
    size = array.shape[axis] // parts
    return lax.dynamic_slice_in_dim(array, index * size, size, axis)


def put_part(part, axis, parts, index):
    shape = list(part.shape)
    shape[axis] = shape[axis] * parts
    return lax.dynamic_update_slice_in_dim(
        jnp.zeros(shape, part.dtype), part, index * part.shape[axis], axis
    )


def layer_forward(stream, weights):
    gain_one, shift_one, w_qkv, qkv_add, w_out, out_shift, gain_two, shift_two, w_up, up_shift, w_down, down_shift = weights
    normed_one = seq_gather(norm_rows(stream, gain_one, shift_one).astype(BF))
    heads = (dot_in(normed_one, w_qkv) + qkv_add).astype(BF)
    outs = [attend_forward(heads[clip]) for clip in range(heads.shape[0])]
    mixed = jnp.stack([pair[0] for pair in outs])
    log_total = jnp.stack([pair[1] for pair in outs])
    attended = stream + (seq_reduce(dot_in(mixed, w_out)) + out_shift)
    normed_two = seq_gather(norm_rows(attended, gain_two, shift_two).astype(BF))
    hidden = dot_in(normed_two, w_up) + up_shift
    activated = jax.nn.gelu(hidden, approximate=False).astype(BF)
    result = attended + (seq_reduce(dot_in(activated, w_down)) + down_shift)
    return (stream, normed_one, heads, log_total, mixed, attended, normed_two, hidden, activated), result


def sum_rows(rows):
    return jnp.sum(rows.astype(F32), axis=(0, 1))


def layer_backward(upstream, weights, state, seq_index, seq_size, fsdp_size):
    gain_one, shift_one, w_qkv, qkv_add, w_out, out_shift, gain_two, shift_two, w_up, up_shift, w_down, down_shift = weights
    stream, normed_one, heads, log_total, mixed, attended, normed_two, hidden, activated = state
    grad_down_local = upstream.astype(BF)
    down_shift_grad = sum_rows(grad_down_local)
    grad_down = seq_gather(grad_down_local)
    w_down_grad = dot_grad(activated, grad_down)
    grad_active = dot_back(grad_down, w_down)
    gelu_pull = jax.vjp(partial(jax.nn.gelu, approximate=False), hidden)[1]
    grad_hidden = gelu_pull(grad_active)[0].astype(BF)
    up_shift_grad = sum_rows(grad_hidden)
    w_up_grad = dot_grad(normed_two, grad_hidden)
    grad_normed_two = seq_reduce(dot_back(grad_hidden, w_up))
    _, pull_two = jax.vjp(norm_rows, attended, gain_two, shift_two)
    grad_attended, gain_two_grad, shift_two_grad = pull_two(grad_normed_two)
    grad_attended = grad_attended + upstream
    grad_out_local = grad_attended.astype(BF)
    out_shift_grad = sum_rows(grad_out_local)
    grad_out = seq_gather(grad_out_local)
    w_out_grad = dot_grad(mixed, grad_out)
    grad_mixed = dot_back(grad_out, w_out).astype(BF)
    grad_projected = jnp.stack(
        [
            attend_backward((heads[clip], log_total[clip], grad_mixed[clip]))
            for clip in range(heads.shape[0])
        ]
    )
    qkv_add_grad = sum_rows(grad_projected)
    w_qkv_grad = dot_grad(normed_one, grad_projected)
    grad_normed_one = seq_reduce(dot_back(grad_projected, w_qkv))
    _, pull_one = jax.vjp(norm_rows, stream, gain_one, shift_one)
    grad_stream, gain_one_grad, shift_one_grad = pull_one(grad_normed_one)
    grad_stream = grad_stream + grad_attended

    out_columns = lax.all_to_all(w_out_grad.astype(BF), "seq", split_axis=1, concat_axis=0, tiled=True)
    big = jnp.concatenate(
        [w_up_grad.astype(BF), w_down_grad.astype(BF), w_qkv_grad.astype(BF), out_columns], axis=1
    )
    local_heads = qkv_add_grad.shape[0] // (3 * HEAD_DIM)
    triple = qkv_add_grad.reshape(local_heads, 3, HEAD_DIM)
    up_parts = put_part(up_shift_grad.reshape(fsdp_size, -1), 1, seq_size, seq_index)
    small = jnp.concatenate(
        [
            gain_one_grad,
            shift_one_grad,
            put_part(triple[:, 0].reshape(-1), 0, seq_size, seq_index),
            put_part(triple[:, 2].reshape(-1), 0, seq_size, seq_index),
            out_shift_grad,
            gain_two_grad,
            shift_two_grad,
            down_shift_grad,
            up_parts.reshape(-1),
        ]
    )
    return grad_stream, big, small


def reduce_big(big):
    owned = lax.psum_scatter(big, "fsdp", scatter_dimension=0, tiled=True)
    return lax.all_gather(owned, "seq", axis=0, tiled=False)


def unpack_big(gathered, sizes):
    up, down, qkv, out = sizes
    spots = [0, up, up + down, up + down + qkv, up + down + qkv + out]
    rows = gathered.shape[1]
    members = [gathered[:, :, spots[i] : spots[i + 1]].astype(F32) for i in range(4)]
    fsdp_size = D // rows
    seq_size = gathered.shape[0]
    w_up = members[0].reshape(seq_size, rows, fsdp_size, -1).transpose(1, 2, 0, 3).reshape(rows, -1)
    w_down = members[1].reshape(seq_size * rows, -1)
    w_qkv = members[2].transpose(1, 0, 2).reshape(rows, -1)
    w_out = members[3].transpose(1, 0, 2).reshape(rows, -1)
    return w_qkv, w_out, w_up, w_down


def attend_forward(packed):
    frames = packed.shape[0]
    local_heads = packed.shape[1] // (3 * HEAD_DIM)
    parts = packed.reshape(frames, local_heads, 3, HEAD_DIM)
    scores = jnp.einsum(
        "qhd,khd->hqk", parts[:, :, 0], parts[:, :, 1], preferred_element_type=jnp.float32
    ) * HEAD_DIM ** (-0.5)
    peak_score = jnp.max(scores, axis=-1, keepdims=True)
    expanded = jnp.exp(scores - peak_score)
    totals = jnp.sum(expanded, axis=-1, keepdims=True)
    weights = (expanded / totals).astype(jnp.bfloat16)
    mixed = jnp.einsum("hqk,khd->qhd", weights, parts[:, :, 2], preferred_element_type=jnp.float32)
    return (
        mixed.reshape(frames, local_heads * HEAD_DIM).astype(jnp.bfloat16),
        (peak_score + jnp.log(totals))[..., 0],
    )


def attend_backward(inputs):
    packed, log_total, incoming = inputs
    frames = packed.shape[0]
    local_heads = packed.shape[1] // (3 * HEAD_DIM)
    parts = packed.reshape(frames, local_heads, 3, HEAD_DIM)
    queries = parts[:, :, 0]
    keys_local = parts[:, :, 1]
    values_local = parts[:, :, 2]
    scale = HEAD_DIM ** (-0.5)
    scores = (
        jnp.einsum("qhd,khd->hqk", queries, keys_local, preferred_element_type=jnp.float32) * scale
    )
    probs = jnp.exp(scores - log_total[..., None])
    incoming_heads = incoming.reshape(frames, local_heads, HEAD_DIM)
    grad_probs = jnp.einsum(
        "qhd,khd->hqk", incoming_heads, values_local, preferred_element_type=jnp.float32
    )
    grad_values = jnp.einsum(
        "hqk,qhd->khd",
        probs.astype(jnp.bfloat16),
        incoming_heads,
        preferred_element_type=jnp.float32,
    )
    grad_scores = (
        probs * (grad_probs - jnp.sum(probs * grad_probs, axis=-1, keepdims=True))
    ).astype(jnp.bfloat16)
    grad_queries = (
        jnp.einsum("hqk,khd->qhd", grad_scores, keys_local, preferred_element_type=jnp.float32)
        * scale
    )
    grad_keys = (
        jnp.einsum("hqk,qhd->khd", grad_scores, queries, preferred_element_type=jnp.float32) * scale
    )
    stacked = jnp.stack([grad_queries, grad_keys, grad_values], axis=2)
    return stacked.reshape(frames, local_heads * 3 * HEAD_DIM).astype(jnp.bfloat16)


def local(
    frames_in,
    norm1_gain,
    norm1_bias,
    qkv_weight,
    qv_bias,
    out_weight,
    out_bias,
    norm2_gain,
    norm2_bias,
    fc1_weight,
    fc1_bias,
    fc2_weight,
    fc2_bias,
    out_cotangent,
):
    shards = (
        norm1_gain,
        norm1_bias,
        qkv_weight,
        qv_bias,
        out_weight,
        out_bias,
        norm2_gain,
        norm2_bias,
        fc1_weight,
        fc1_bias,
        fc2_weight,
        fc2_bias,
    )
    layer_count = qkv_weight.shape[0]
    fsdp_size = lax.axis_size("fsdp")
    seq_size = lax.axis_size("seq")
    seq_index = lax.axis_index("seq")
    owner = lax.axis_index("fsdp")
    rows = qkv_weight.shape[1]
    part_rows = fc1_bias.shape[1] // seq_size
    hidden_local = fsdp_size * part_rows

    small_in = jnp.concatenate(
        [norm1_gain, norm1_bias, qv_bias[:, 0], qv_bias[:, 1], out_bias, norm2_gain, norm2_bias, fc2_bias, fc1_bias],
        axis=1,
    )
    small_all = lax.all_gather(small_in.reshape(-1), "fsdp", axis=0, tiled=False)
    small_all = small_all.reshape(fsdp_size, layer_count, -1).astype(F32)

    weights = []
    for level in range(layer_count):
        up_part = take_part(fc1_weight[level].reshape(rows, fsdp_size, -1), 2, seq_size, seq_index)
        packed = jnp.concatenate(
            [
                up_part.reshape(rows, hidden_local),
                take_part(fc2_weight[level], 0, seq_size, seq_index),
                take_part(qkv_weight[level], 1, seq_size, seq_index),
                out_weight[level],
            ],
            axis=1,
        )
        packed = lax.all_gather(packed, "fsdp", axis=0, tiled=True)
        third = 3 * D // seq_size
        w_up = packed[:, :hidden_local]
        w_down = packed[:, hidden_local : hidden_local + D]
        w_qkv = packed[:, hidden_local + D : hidden_local + D + third]
        w_out = take_part(packed[:, hidden_local + D + third :], 0, seq_size, seq_index)
        pieces = small_all[:, level]
        vectors = [pieces[:, i * rows : (i + 1) * rows].reshape(D) for i in range(8)]
        gain_one, shift_one, query_add, value_add, out_shift, gain_two, shift_two, down_shift = vectors
        up_shift = take_part(pieces[:, 8 * rows :], 1, seq_size, seq_index).reshape(hidden_local)
        qkv_add = take_part(qkv_shift(jnp.stack([query_add, value_add])), 0, seq_size, seq_index)
        weights.append(
            (gain_one, shift_one, w_qkv, qkv_add, w_out, out_shift, gain_two, shift_two, w_up, up_shift, w_down, down_shift)
        )

    stream = frames_in.astype(F32)
    saved = []
    for level in range(layer_count):
        kept, stream = layer_forward(stream, weights[level])
        saved.append(kept)
    frames_out = stream.astype(BF)
    upstream = out_cotangent.astype(F32)
    reduced = [None] * layer_count
    smalls = [None] * layer_count
    for level in reversed(range(layer_count)):
        upstream, big, small = layer_backward(
            upstream, weights[level], saved[level], seq_index, seq_size, fsdp_size
        )
        smalls[level] = small
        reduced[level] = unpack_big(
            reduce_big(big), (hidden_local, D, 3 * D // seq_size, D // seq_size)
        )
    small_sum = lax.psum(jnp.stack(smalls), ("seq", "fsdp"))
    vectors = [take_part(small_sum[:, i * D : (i + 1) * D], 1, fsdp_size, owner) for i in range(8)]
    up_sum = take_part(small_sum[:, 8 * D :], 1, fsdp_size, owner)
    qkv_grad, out_grad, up_grad, down_grad = [
        jnp.stack([reduced[level][member] for level in range(layer_count)]) for member in range(4)
    ]
    return (
        frames_out,
        upstream,
        vectors[0],
        vectors[1],
        qkv_grad,
        jnp.stack([vectors[2], vectors[3]], axis=1),
        out_grad,
        vectors[4],
        vectors[5],
        vectors[6],
        up_grad,
        up_sum,
        down_grad,
        vectors[7],
    )


def solution(mesh):
    in_specs = (
        P("fsdp", "seq", None),
        P(None, "fsdp"),
        P(None, "fsdp"),
        P(None, "fsdp", None),
        P(None, None, "fsdp"),
        P(None, "fsdp", None),
        P(None, "fsdp"),
        P(None, "fsdp"),
        P(None, "fsdp"),
        P(None, "fsdp", None),
        P(None, "fsdp"),
        P(None, "fsdp", None),
        P(None, "fsdp"),
        P("fsdp", "seq", None),
    )
    out_specs = (
        P("fsdp", "seq", None),
        P("fsdp", "seq", None),
        P(None, "fsdp"),
        P(None, "fsdp"),
        P(None, "fsdp", None),
        P(None, None, "fsdp"),
        P(None, "fsdp", None),
        P(None, "fsdp"),
        P(None, "fsdp"),
        P(None, "fsdp"),
        P(None, "fsdp", None),
        P(None, "fsdp"),
        P(None, "fsdp", None),
        P(None, "fsdp"),
    )
    return jax.shard_map(local, mesh=mesh, in_specs=in_specs, out_specs=out_specs, check_vma=False)
```

time: 2250 us -> 1100 us (0.49)
  waiting for transfers between devices: 1390 us -> 753 us
  blocking collectives: 251 us -> 32.3 us
  local copies, waits for them, and re-layouts: 271 us -> 74.5 us
  other arithmetic: 124 us -> 69.5 us
    reduce_scatter x8 -> x10, waiting for transfers between devices: 1020 us -> 316 us  [the longest x8 219 us: seq_reduce(): lax.psum_scatter(partial_sum.astype(BF), 'seq', scatter_dimension=1, tile...]
    unnamed x24 -> x23, waiting for transfers between devices: 151 us -> 0.89 us
    all_gather x8 -> x12, waiting for transfers between devices: 196 us -> 316 us  [the longest x2 157 us: local(): packed = lax.all_gather(packed, 'fsdp', axis=0, tiled=True)]
    psum x0 -> x1, waiting for transfers between devices: none -> 109 us  [local(): small_sum = lax.psum(jnp.stack(smalls), ('seq', 'fsdp'))]
    all_gather x4 -> x1, blocking collectives: 116 us -> 32.3 us  [local(): lax.all_gather(small_in.reshape(-1), 'fsdp', axis=0, tiled=False)]
    unnamed x2 -> x0, blocking collectives: 75.9 us -> none
    concatenate x2 -> x5, local copies, waits for them, and re-layouts: 71 us -> 2.93 us  [the longest x2 2.04 us: local(): jnp.concatenate([up_part.reshape(rows, hidden_local), take_part(fc2_weigh...]
    unnamed x342 -> x207, local copies, waits for them, and re-layouts: 94.3 us -> 27.4 us
  transfers between devices with their start and end apart: 25 -> 25, of which waited for: 18 -> 24; matrix products, arithmetic and copies ran while one was open for 12% -> 12% of each run, Pallas kernels for 0% -> 0%
where the time goes in v1:
time: 1100 us; the launch traced here: 1090 us
  waiting for transfers between devices  753 us (68%)
  matrix products  139 us (13%)
  local copies, waits for them, and re-layouts  74.5 us (7%)
  other arithmetic  69.5 us (6%)
  blocking collectives  32.3 us (3%)
  between operations  15.9 us (1%)
    reduce_scatter x8, waiting for transfers between devices, seq_reduce(): lax.psum_scatter(partial_sum.astype(BF), 'seq', scatter_dimension=1, tile...  219 us
    all_gather x2, waiting for transfers between devices, local(): packed = lax.all_gather(packed, 'fsdp', axis=0, tiled=True)  157 us
    all_gather x8, waiting for transfers between devices, seq_gather(): return lax.all_gather(block, 'seq', axis=1, tiled=True)  119 us
    psum x1, waiting for transfers between devices, local(): small_sum = lax.psum(jnp.stack(smalls), ('seq', 'fsdp'))  109 us
    reduce_scatter x2, waiting for transfers between devices, reduce_big(): owned = lax.psum_scatter(big, 'fsdp', scatter_dimension=0, tiled=True)  96.8 us
    dot_general x8, matrix products, dot_in(): return jnp.einsum('cfi,io->cfo', rows, matrix, preferred_element_type=F32)  40.2 us
    all_gather x2, waiting for transfers between devices, reduce_big(): return lax.all_gather(owned, 'seq', axis=0, tiled=False)  39.4 us
    dot_general x8, matrix products, dot_back(): return jnp.einsum('cfo,io->cfi', rows, matrix, preferred_element_type=F32)  32.4 us
  transfers between devices with their start and end apart: 25, of which 24 were waited for; matrix products, arithmetic and copies ran while one was open for 12% of the time, Pallas kernels for 0%

profile of v1, /device:TPU:0, one launch (start us, length us, event | category | flops | bytes accessed | tf_op | source)
XLA Modules:
  0.0 1093.3 jit_solution(3094065393402558453)
XLA Ops:
  11.4 32.3 %all-gather.2 = bf16[8,1,2304]{2,1,0:T(2,128)(2,1)S(1)} all-gather(bf16[1,1,2304]{2,1,0:T(2,128)(2,1)S(1)} %reshape.700), channel_id=1, replica_groups=mesh['seq'=4,'fsdp'=8] {'fsdp'}, dimensions={0}, use_global_device_ids=true | all-gather | bytes 41472 | tf_op jit(solution)/shard_map/all_gather | solution.py:262
  51.9 15.1 %all-gather.16.cloned.1.call-done = bf16[1,1024,768]{2,1,0:T(8,128)(2,1)} async-done(((bf16[1,256,768]{2,1,0:T(8,128)(2,1)}), bf16[1,1024,768]{2,1,0:T(8,128)(2,1)}) %all-gather.16.cloned.1.call-update) | async-done | bytes 1572880 | tf_op jit(solution)/shard_map/all_gather | solution.py:36
  67.1 80.3 %all-gather.18.cloned.1.call-done = bf16[768,2880]{1,0:T(8,128)(2,1)} async-done(((bf16[96,2880]{1,0:T(8,128)(2,1)}), bf16[768,2880]{1,0:T(8,128)(2,1)}) %all-gather.18.cloned.1.call-update) | async-done | bytes 4423696 | tf_op jit(solution)/shard_map/all_gather | solution.py:277
  164.3 26.2 %reduce-scatter.15.cloned.1.call-done = bf16[1,256,768]{2,1,0:T(8,128)(2,1)} async-done(((bf16[1,1024,768]{2,1,0:T(8,128)(2,1)}), bf16[1,256,768]{2,1,0:T(8,128)(2,1)}) %reduce-scatter.15.cloned.1.call-update) | async-done | bytes 393232 | tf_op jit(solution)/shard_map/reduce_scatter | solution.py:40
  195.7 19.1 %all-gather.20.cloned.1.call-done = bf16[1,1024,768]{2,1,0:T(8,128)(2,1)} async-done(((bf16[1,256,768]{2,1,0:T(8,128)(2,1)}), bf16[1,1024,768]{2,1,0:T(8,128)(2,1)}) %all-gather.20.cloned.1.call-update) | async-done | bytes 1572880 | tf_op jit(solution)/shard_map/all_gather | solution.py:36
  214.9 11.4 %multiply_convert_fusion.3 = (bf16[1024,768]{1,0:T(8,128)(2,1)S(1)}, f32[1024,768]{1,0:T(8,128)}, f32[1024,768]{1,0:T(8,128)}) fusion(f32[768]{0:T(1024)S(1)} %add.284, bf16[768,2880]{1,0:T(8,128)(2,1)} %all-gather.18.cloned.1.call-done, bf16[1,1024,768]{2,1,0:T(8,128)(2,1)} %all-gather.20.cloned.1.call-done), kind=kOutput, calls=%fused_computation.51 | convolution fusion | flops 1259864064 | bytes 10619904 | tf_op jit(solution)/shard_map/cfi,io->cfo/dot_general | solution.py:45
  234.1 25.5 %reduce-scatter.17.cloned.1.call-done = bf16[1,256,768]{2,1,0:T(8,128)(2,1)} async-done(((bf16[1,1024,768]{2,1,0:T(8,128)(2,1)}), bf16[1,256,768]{2,1,0:T(8,128)(2,1)}) %reduce-scatter.17.cloned.1.call-update) | async-done | bytes 393232 | tf_op jit(solution)/shard_map/reduce_scatter | solution.py:40
  262.6 77.1 %all-gather.24.cloned.1.call-done = bf16[768,2880]{1,0:T(8,128)(2,1)} async-done(((bf16[96,2880]{1,0:T(8,128)(2,1)}), bf16[768,2880]{1,0:T(8,128)(2,1)}) %all-gather.24.cloned.1.call-update) | async-done | bytes 4423696 | tf_op jit(solution)/shard_map/all_gather | solution.py:277
  341.6 18.1 %all-gather.22.cloned.1.call-done = bf16[1,1024,768]{2,1,0:T(8,128)(2,1)} async-done(((bf16[1,256,768]{2,1,0:T(8,128)(2,1)}), bf16[1,1024,768]{2,1,0:T(8,128)(2,1)}) %all-gather.22.cloned.1.call-update) | async-done | bytes 1572880 | tf_op jit(solution)/shard_map/all_gather | solution.py:36
  374.5 28.1 %reduce-scatter.19.cloned.1.call-done = bf16[1,256,768]{2,1,0:T(8,128)(2,1)} async-done(((bf16[1,1024,768]{2,1,0:T(8,128)(2,1)}), bf16[1,256,768]{2,1,0:T(8,128)(2,1)}) %reduce-scatter.19.cloned.1.call-update) | async-done | bytes 393232 | tf_op jit(solution)/shard_map/reduce_scatter | solution.py:40
  405.9 18.8 %all-gather.26.cloned.1.call-done = bf16[1,1024,768]{2,1,0:T(8,128)(2,1)} async-done(((bf16[1,256,768]{2,1,0:T(8,128)(2,1)}), bf16[1,1024,768]{2,1,0:T(8,128)(2,1)}) %all-gather.26.cloned.1.call-update) | async-done | bytes 1572880 | tf_op jit(solution)/shard_map/all_gather | solution.py:36
  424.7 11.6 %multiply_convert_fusion.2 = (bf16[1024,768]{1,0:T(8,128)(2,1)}, f32[1024,768]{1,0:T(8,128)}, f32[1024,768]{1,0:T(8,128)}) fusion(f32[768]{0:T(1024)S(1)} %add.305, bf16[768,2880]{1,0:T(8,128)(2,1)} %all-gather.24.cloned.1.call-done, bf16[1,1024,768]{2,1,0:T(8,128)(2,1)} %all-gather.26.cloned.1.call-done), kind=kOutput, calls=%fused_computation.38 | convolution fusion | flops 1259864064 | bytes 10619904 | tf_op jit(solution)/shard_map/cfi,io->cfo/dot_general | solution.py:45
  461.9 23.8 %reduce-scatter.23.cloned.1.call-done = bf16[1,256,768]{2,1,0:T(8,128)(2,1)} async-done(((bf16[1,1024,768]{2,1,0:T(8,128)(2,1)}), bf16[1,256,768]{2,1,0:T(8,128)(2,1)}) %reduce-scatter.23.cloned.1.call-update) | async-done | bytes 393232 | tf_op jit(solution)/shard_map/reduce_scatter | solution.py:40
  488.2 28.7 %reduce-scatter.21.cloned.1.call-done = bf16[1,256,768]{2,1,0:T(8,128)(2,1)} async-done(((bf16[1,1024,768]{2,1,0:T(8,128)(2,1)}), bf16[1,256,768]{2,1,0:T(8,128)(2,1)}) %reduce-scatter.21.cloned.1.call-update) | async-done | bytes 393232 | tf_op jit(solution)/shard_map/reduce_scatter | solution.py:40
  521.9 18.6 %all-gather.30.cloned.1.call-done = bf16[1,1024,768]{2,1,0:T(8,128)(2,1)} async-done(((bf16[1,256,768]{2,1,0:T(8,128)(2,1)}), bf16[1,1024,768]{2,1,0:T(8,128)(2,1)}) %all-gather.30.cloned.1.call-update) | async-done | bytes 1572880 | tf_op jit(solution)/shard_map/all_gather | solution.py:36
  575.3 28.3 %reduce-scatter.25.cloned.1.call-done = bf16[1,256,768]{2,1,0:T(8,128)(2,1)} async-done(((bf16[1,1024,768]{2,1,0:T(8,128)(2,1)}), bf16[1,256,768]{2,1,0:T(8,128)(2,1)}) %reduce-scatter.25.cloned.1.call-update) | async-done | bytes 393232 | tf_op jit(solution)/shard_map/reduce_scatter | solution.py:40
  610.5 19.6 %all-gather.32.cloned.1.call-done = bf16[1,1024,768]{2,1,0:T(8,128)(2,1)} async-done(((bf16[1,256,768]{2,1,0:T(8,128)(2,1)}), bf16[1,1024,768]{2,1,0:T(8,128)(2,1)}) %all-gather.32.cloned.1.call-update) | async-done | bytes 1572880 | tf_op jit(solution)/shard_map/all_gather | solution.py:36
  641.7 28.3 %reduce-scatter.27.cloned.1.call-done = bf16[1,256,768]{2,1,0:T(8,128)(2,1)} async-done(((bf16[1,1024,768]{2,1,0:T(8,128)(2,1)}), bf16[1,256,768]{2,1,0:T(8,128)(2,1)}) %reduce-scatter.27.cloned.1.call-update) | async-done | bytes 393232 | tf_op jit(solution)/shard_map/reduce_scatter | solution.py:40
  770.2 18.1 %reduce-scatter.33.cloned.1.call-done = bf16[96,2304]{1,0:T(8,128)(2,1)} async-done(((bf16[768,2304]{1,0:T(8,128)(2,1)}), bf16[96,2304]{1,0:T(8,128)(2,1)}) %reduce-scatter.33.cloned.1.call-update) | async-done | bytes 442384 | tf_op jit(solution)/shard_map/reduce_scatter | solution.py:146
  789.0 30.4 %reduce-scatter.29.cloned.1.call-done = bf16[1,256,768]{2,1,0:T(8,128)(2,1)} async-done(((bf16[1,1024,768]{2,1,0:T(8,128)(2,1)}), bf16[1,256,768]{2,1,0:T(8,128)(2,1)}) %reduce-scatter.29.cloned.1.call-update) | async-done | bytes 393232 | tf_op jit(solution)/shard_map/reduce_scatter | solution.py:40
  823.1 78.7 %reduce-scatter.31.cloned.1.call-done = bf16[96,2304]{1,0:T(8,128)(2,1)} async-done(((bf16[768,2304]{1,0:T(8,128)(2,1)}), bf16[96,2304]{1,0:T(8,128)(2,1)}) %reduce-scatter.31.cloned.1.call-update) | async-done | bytes 442384 | tf_op jit(solution)/shard_map/reduce_scatter | solution.py:146
  901.8 21.9 %all-gather.38.cloned.1.call-done = bf16[384,2304]{1,0:T(8,128)(2,1)} async-done(((bf16[96,2304]{1,0:T(8,128)(2,1)}), bf16[384,2304]{1,0:T(8,128)(2,1)}) %all-gather.38.cloned.1.call-update) | async-done | bytes 1769488 | tf_op jit(solution)/shard_map/all_gather | solution.py:147
  938.7 109.0 %all-reduce.2.cloned.1.call-done = f32[2,9216]{1,0:T(2,128)} async-done(((f32[2,9216]{1,0:T(2,128)}), f32[2,9216]{1,0:T(2,128)}) %all-reduce.2.cloned.1.call-update) | async-done | bytes 73744 | tf_op jit(solution)/shard_map/psum | solution.py:309
  1054.3 17.6 %all-gather.36.cloned.1.call-done = bf16[384,2304]{1,0:T(8,128)(2,1)} async-done(((bf16[96,2304]{1,0:T(8,128)(2,1)}), bf16[384,2304]{1,0:T(8,128)(2,1)}) %all-gather.36.cloned.1.call-update) | async-done | bytes 1769488 | tf_op jit(solution)/shard_map/all_gather | solution.py:147
  (470 shorter events, 290.8 us)
Async XLA Ops:
  7.2 59.9 %all-gather.16.cloned.1.call-start = ((), (), s32[]{:S(2)}) async-start(), calls=%async_computation.12 | async-start | bytes 1966080 | tf_op jit(solution)/shard_map/all_gather | solution.py:36
  46.3 101.0 %all-gather.18.cloned.1.call-start = ((), (), s32[]{:S(2)}) async-start(), calls=%async_computation.13 | async-start | bytes 5087232 | tf_op jit(solution)/shard_map/all_gather | solution.py:277
  51.2 139.4 %reduce-scatter.15.cloned.1.call-start = ((), (), s32[]{:S(2)}) async-start(), calls=%async_computation.14 | async-start | bytes 1966080 | tf_op jit(solution)/shard_map/reduce_scatter | solution.py:40
  164.1 50.8 %all-gather.20.cloned.1.call-start = ((), (), s32[]{:S(2)}) async-start(), calls=%async_computation.15 | async-start | bytes 1966080 | tf_op jit(solution)/shard_map/all_gather | solution.py:36
  195.1 64.6 %reduce-scatter.17.cloned.1.call-start = ((), (), s32[]{:S(2)}) async-start(), calls=%async_computation.16 | async-start | bytes 1966080 | tf_op jit(solution)/shard_map/reduce_scatter | solution.py:40
  231.3 108.4 %all-gather.24.cloned.1.call-start = ((), (), s32[]{:S(2)}) async-start(), calls=%async_computation.18 | async-start | bytes 5087232 | tf_op jit(solution)/shard_map/all_gather | solution.py:277
  233.9 125.9 %all-gather.22.cloned.1.call-start = ((), (), s32[]{:S(2)}) async-start(), calls=%async_computation.17 | async-start | bytes 1966080 | tf_op jit(solution)/shard_map/all_gather | solution.py:36
  262.2 140.4 %reduce-scatter.19.cloned.1.call-start = ((), (), s32[]{:S(2)}) async-start(), calls=%async_computation.19 | async-start | bytes 1966080 | tf_op jit(solution)/shard_map/reduce_scatter | solution.py:40
  374.2 50.6 %all-gather.26.cloned.1.call-start = ((), (), s32[]{:S(2)}) async-start(), calls=%async_computation.20 | async-start | bytes 1966080 | tf_op jit(solution)/shard_map/all_gather | solution.py:36
  404.9 41.0 %all-gather.28.cloned.1.call-start = ((), (), s32[]{:S(2)}) async-start(), calls=%async_computation.22 | async-start | bytes 1966080 | tf_op jit(solution)/shard_map/all_gather | solution.py:36
  405.5 80.2 %reduce-scatter.23.cloned.1.call-start = ((), (), s32[]{:S(2)}) async-start(), calls=%async_computation.23 | async-start | bytes 1966080 | tf_op jit(solution)/shard_map/reduce_scatter | solution.py:40
  457.4 59.5 %reduce-scatter.21.cloned.1.call-start = ((), (), s32[]{:S(2)}) async-start(), calls=%async_computation.21 | async-start | bytes 1966080 | tf_op jit(solution)/shard_map/reduce_scatter | solution.py:40
  461.7 78.7 %all-gather.30.cloned.1.call-start = ((), (), s32[]{:S(2)}) async-start(), calls=%async_computation.24 | async-start | bytes 1966080 | tf_op jit(solution)/shard_map/all_gather | solution.py:36
  520.6 82.9 %reduce-scatter.25.cloned.1.call-start = ((), (), s32[]{:S(2)}) async-start(), calls=%async_computation.25 | async-start | bytes 1966080 | tf_op jit(solution)/shard_map/reduce_scatter | solution.py:40
  575.2 54.9 %all-gather.32.cloned.1.call-start = ((), (), s32[]{:S(2)}) async-start(), calls=%async_computation.26 | async-start | bytes 1966080 | tf_op jit(solution)/shard_map/all_gather | solution.py:36
  610.3 59.6 %reduce-scatter.27.cloned.1.call-start = ((), (), s32[]{:S(2)}) async-start(), calls=%async_computation.27 | async-start | bytes 1966080 | tf_op jit(solution)/shard_map/reduce_scatter | solution.py:40
  641.6 68.2 %all-gather.34.cloned.1.call-start = ((), (), s32[]{:S(2)}) async-start(), calls=%async_computation.28 | async-start | bytes 1966080 | tf_op jit(solution)/shard_map/all_gather | solution.py:36
  684.3 15.0 %all-to-all-start.1 = ((bf16[192,4,192]{0,2,1:T(8,128)(2,1)}), bf16[192,4,192]{0,2,1:T(8,128)(2,1)S(1)}, u32[]{:S(2)}, u32[]{:S(2)}) async-start(bf16[192,4,192]{0,2,1:T(8,128)(2,1)} %bitcast.61), calls=%async_computation.9 | async-start | bytes 786432 | tf_op jit(solution)/shard_map/all_to_all | solution.py:122
  687.8 100.5 %reduce-scatter.33.cloned.1.call-start = ((), (), s32[]{:S(2)}) async-start(), calls=%async_computation.34 | async-start | bytes 3981312 | tf_op jit(solution)/shard_map/reduce_scatter | solution.py:146
  709.0 110.3 %reduce-scatter.29.cloned.1.call-start = ((), (), s32[]{:S(2)}) async-start(), calls=%async_computation.29 | async-start | bytes 1966080 | tf_op jit(solution)/shard_map/reduce_scatter | solution.py:40
  751.1 150.7 %reduce-scatter.31.cloned.1.call-start = ((), (), s32[]{:S(2)}) async-start(), calls=%async_computation.33 | async-start | bytes 3981312 | tf_op jit(solution)/shard_map/reduce_scatter | solution.py:146
  768.4 155.3 %all-gather.38.cloned.1.call-start = ((), (), s32[]{:S(2)}) async-start(), calls=%async_computation.32 | async-start | bytes 2211840 | tf_op jit(solution)/shard_map/all_gather | solution.py:147
  788.3 259.3 %all-reduce.2.cloned.1.call-start = ((), (), s32[]{:S(2)}) async-start(), calls=%async_computation.30 | async-start | bytes 147456 | tf_op jit(solution)/shard_map/psum | solution.py:309
  823.1 248.8 %all-gather.36.cloned.1.call-start = ((), (), s32[]{:S(2)}) async-start(), calls=%async_computation.31 | async-start | bytes 2211840 | tf_op jit(solution)/shard_map/all_gather | solution.py:147
  (93 other events, 1574.4 us)
Sparse Core Ops, SparseCore 0:
  46.5 20.5 all-gather.15
  69.8 77.4 all-gather.17
  164.2 26.3 reduce-scatter.14
  195.2 19.6 all-gather.19
  231.4 28.1 reduce-scatter.16
  262.2 77.4 all-gather.23
  341.9 17.8 all-gather.21
  374.3 28.1 reduce-scatter.18
  405.0 19.6 all-gather.25
  426.2 19.6 all-gather.27
  457.5 28.1 reduce-scatter.22
  488.7 28.1 reduce-scatter.20
  520.8 19.6 all-gather.29
  575.4 28.1 reduce-scatter.24
  610.4 19.6 all-gather.31
  641.8 28.1 reduce-scatter.26
  677.0 23.7 all-gather.33
  709.2 79.0 reduce-scatter.32
  791.6 27.7 reduce-scatter.28
  822.8 78.9 reduce-scatter.30
  903.4 20.2 all-gather.37
  929.3 118.3 all-reduce.1
  1049.2 22.6 all-gather.35

commit v2 on v1

--- a/solution.py
+++ b/solution.py
@@ -4,6 +4,8 @@
 import jax
 import jax.numpy as jnp
 from jax import lax
+from jax.experimental import pallas as pl
+from jax.experimental.pallas import tpu as pltpu
 from jax.sharding import PartitionSpec as P
 
 D = 768
@@ -32,13 +34,121 @@
 F32 = jnp.float32
 
 
+MESH_ID = pl.DeviceIdType.MESH
+
+
+def partners():
+    me = lax.axis_index("seq")
+    core = me + 1 - 2 * lax.rem(me, 2)
+    across = lax.rem(me + 2, 4)
+    return me, core, across, lax.rem(core + 2, 4)
+
+
+def greet(core, across):
+    barrier = pltpu.get_barrier_semaphore()
+    for other in (core, across):
+        pl.semaphore_signal(barrier, inc=1, device_id={"seq": other}, device_id_type=MESH_ID)
+    pl.semaphore_wait(barrier, 2)
+
+
+def send(src, dst, send_sem, recv_sem, other):
+    return pltpu.make_async_remote_copy(
+        src_ref=src,
+        dst_ref=dst,
+        send_sem=send_sem,
+        recv_sem=recv_sem,
+        device_id={"seq": other},
+        device_id_type=MESH_ID,
+    )
+
+
+def gather_kernel(block_ref, whole_ref, land, send_sem, recv_sem):
+    me, core, across, far = partners()
+    greet(core, across)
+    over = send(block_ref, land.at[1], send_sem.at[1], recv_sem.at[1], across)
+    over.start()
+    beside = send(block_ref, land.at[0], send_sem.at[0], recv_sem.at[0], core)
+    beside.start()
+    whole_ref[me] = block_ref[...]
+    over.wait_recv()
+    relay = send(land.at[1], land.at[2], send_sem.at[2], recv_sem.at[2], core)
+    relay.start()
+    whole_ref[across] = land[1]
+    beside.wait_recv()
+    whole_ref[core] = land[0]
+    relay.wait_recv()
+    whole_ref[far] = land[2]
+    over.wait_send()
+    beside.wait_send()
+    relay.wait_send()
+
+
+def reduce_kernel(parts_ref, total_ref, land, pair, send_sem, recv_sem):
+    me, core, across, far = partners()
+    greet(core, across)
+    first = send(parts_ref.at[far], land.at[0], send_sem.at[0], recv_sem.at[0], core)
+    first.start()
+    second = send(parts_ref.at[core], land.at[1], send_sem.at[1], recv_sem.at[1], core)
+    second.start()
+    first.wait_recv()
+    pair[...] = (parts_ref[across].astype(F32) + land[0].astype(F32)).astype(BF)
+    last = send(pair, land.at[2], send_sem.at[2], recv_sem.at[2], across)
+    last.start()
+    second.wait_recv()
+    total_ref[...] = parts_ref[me].astype(F32) + land[1].astype(F32)
+    last.wait_recv()
+    total_ref[...] += land[2].astype(F32)
+    first.wait_send()
+    second.wait_send()
+    last.wait_send()
+
+
+def kernel_params(number):
+    return pltpu.CompilerParams(
+        collective_id=number, has_side_effects=True, vmem_limit_bytes=24 * 1024 * 1024
+    )
+
+
 def seq_gather(block):
-    return lax.all_gather(block, "seq", axis=1, tiled=True)
+    clips, frames, width = block.shape
+    rows = clips * frames
+    whole = pl.pallas_call(
+        gather_kernel,
+        out_shape=jax.ShapeDtypeStruct((4, rows, width), BF),
+        in_specs=[pl.BlockSpec(memory_space=pltpu.VMEM)],
+        out_specs=pl.BlockSpec(memory_space=pltpu.VMEM),
+        scratch_shapes=[
+            pltpu.VMEM((3, rows, width), BF),
+            pltpu.SemaphoreType.DMA((3,)),
+            pltpu.SemaphoreType.DMA((3,)),
+        ],
+        compiler_params=kernel_params(0),
+        cost_estimate=pl.CostEstimate(flops=0, bytes_accessed=16 * rows * width, transcendentals=0),
+    )(block.reshape(rows, width))
+    whole = whole.reshape(4, clips, frames, width).swapaxes(0, 1)
+    return whole.reshape(clips, 4 * frames, width)
 
 
 def seq_reduce(partial_sum):
-    summed = lax.psum_scatter(partial_sum.astype(BF), "seq", scatter_dimension=1, tiled=True)
-    return summed.astype(F32)
+    clips, all_frames, width = partial_sum.shape
+    frames = all_frames // 4
+    rows = clips * frames
+    parts = partial_sum.astype(BF).reshape(clips, 4, frames, width).swapaxes(0, 1)
+    total = pl.pallas_call(
+        reduce_kernel,
+        out_shape=jax.ShapeDtypeStruct((rows, width), F32),
+        in_specs=[pl.BlockSpec(memory_space=pltpu.VMEM)],
+        out_specs=pl.BlockSpec(memory_space=pltpu.VMEM),
+        scratch_shapes=[
+            pltpu.VMEM((3, rows, width), BF),
+            pltpu.VMEM((rows, width), BF),
+            pltpu.SemaphoreType.DMA((3,)),
+            pltpu.SemaphoreType.DMA((3,)),
+        ],
+        compiler_params=kernel_params(1),
+        cost_estimate=pl.CostEstimate(flops=0, bytes_accessed=16 * rows * width, transcendentals=0),
+    )(parts.reshape(4, rows, width))
+    return total.reshape(clips, frames, width)
 
 
 def dot_in(rows, matrix):
@@ -120,13 +230,10 @@
     grad_stream = grad_stream + grad_attended
 
     out_columns = lax.all_to_all(w_out_grad.astype(BF), "seq", split_axis=1, concat_axis=0, tiled=True)
-    big = jnp.concatenate(
-        [w_up_grad.astype(BF), w_down_grad.astype(BF), w_qkv_grad.astype(BF), out_columns], axis=1
-    )
     local_heads = qkv_add_grad.shape[0] // (3 * HEAD_DIM)
     triple = qkv_add_grad.reshape(local_heads, 3, HEAD_DIM)
     up_parts = put_part(up_shift_grad.reshape(fsdp_size, -1), 1, seq_size, seq_index)
-    small = jnp.concatenate(
+    small = jnp.stack(
         [
             gain_one_grad,
             shift_one_grad,
@@ -136,10 +243,16 @@
             gain_two_grad,
             shift_two_grad,
             down_shift_grad,
-            up_parts.reshape(-1),
-        ]
-    )
-    return grad_stream, big, small
+        ],
+        axis=1,
+    )
+    small = jnp.concatenate([small, up_parts.reshape(D, -1)], axis=1).astype(BF)
+    small = jnp.pad(small, ((0, 0), (0, 128 - small.shape[1])))
+    big = jnp.concatenate(
+        [w_up_grad.astype(BF), w_down_grad.astype(BF), w_qkv_grad.astype(BF), out_columns, small],
+        axis=1,
+    )
+    return grad_stream, big
 
 
 def reduce_big(big):
@@ -158,7 +271,8 @@
     w_down = members[1].reshape(seq_size * rows, -1)
     w_qkv = members[2].transpose(1, 0, 2).reshape(rows, -1)
     w_out = members[3].transpose(1, 0, 2).reshape(rows, -1)
-    return w_qkv, w_out, w_up, w_down
+    small = jnp.sum(gathered[:, :, spots[4] :].astype(F32), axis=0)
+    return w_qkv, w_out, w_up, w_down, small
 
 
 def attend_forward(packed):
@@ -250,40 +364,48 @@
     fsdp_size = lax.axis_size("fsdp")
     seq_size = lax.axis_size("seq")
     seq_index = lax.axis_index("seq")
-    owner = lax.axis_index("fsdp")
     rows = qkv_weight.shape[1]
     part_rows = fc1_bias.shape[1] // seq_size
     hidden_local = fsdp_size * part_rows
 
-    small_in = jnp.concatenate(
-        [norm1_gain, norm1_bias, qv_bias[:, 0], qv_bias[:, 1], out_bias, norm2_gain, norm2_bias, fc2_bias, fc1_bias],
-        axis=1,
-    )
-    small_all = lax.all_gather(small_in.reshape(-1), "fsdp", axis=0, tiled=False)
-    small_all = small_all.reshape(fsdp_size, layer_count, -1).astype(F32)
-
     weights = []
     for level in range(layer_count):
         up_part = take_part(fc1_weight[level].reshape(rows, fsdp_size, -1), 2, seq_size, seq_index)
+        small = jnp.stack(
+            [
+                norm1_gain[level],
+                norm1_bias[level],
+                qv_bias[level, 0],
+                qv_bias[level, 1],
+                out_bias[level],
+                norm2_gain[level],
+                norm2_bias[level],
+                fc2_bias[level],
+            ],
+            axis=1,
+        )
+        small = jnp.concatenate([small, fc1_bias[level].reshape(rows, -1)], axis=1)
+        small = jnp.pad(small, ((0, 0), (0, 128 - small.shape[1])))
+        lead = jnp.concatenate([small, take_part(qkv_weight[level], 1, seq_size, seq_index)], axis=1)
+        lead = lax.all_gather(lead, "fsdp", axis=0, tiled=True)
         packed = jnp.concatenate(
             [
                 up_part.reshape(rows, hidden_local),
                 take_part(fc2_weight[level], 0, seq_size, seq_index),
-                take_part(qkv_weight[level], 1, seq_size, seq_index),
                 out_weight[level],
             ],
             axis=1,
         )
         packed = lax.all_gather(packed, "fsdp", axis=0, tiled=True)
-        third = 3 * D // seq_size
         w_up = packed[:, :hidden_local]
         w_down = packed[:, hidden_local : hidden_local + D]
-        w_qkv = packed[:, hidden_local + D : hidden_local + D + third]
-        w_out = take_part(packed[:, hidden_local + D + third :], 0, seq_size, seq_index)
-        pieces = small_all[:, level]
-        vectors = [pieces[:, i * rows : (i + 1) * rows].reshape(D) for i in range(8)]
+        w_qkv = lead[:, 128:]
+        w_out = take_part(packed[:, hidden_local + D :], 0, seq_size, seq_index)
+        pieces = lead[:, :12].astype(F32)
+        vectors = [pieces[:, i] for i in range(8)]
         gain_one, shift_one, query_add, value_add, out_shift, gain_two, shift_two, down_shift = vectors
-        up_shift = take_part(pieces[:, 8 * rows :], 1, seq_size, seq_index).reshape(hidden_local)
+        up_shift = take_part(pieces[:, 8:].reshape(fsdp_size, -1), 1, seq_size, seq_index)
+        up_shift = up_shift.reshape(hidden_local)
         qkv_add = take_part(qkv_shift(jnp.stack([query_add, value_add])), 0, seq_size, seq_index)
         weights.append(
             (gain_one, shift_one, w_qkv, qkv_add, w_out, out_shift, gain_two, shift_two, w_up, up_shift, w_down, down_shift)
@@ -297,21 +419,18 @@
     frames_out = stream.astype(BF)
     upstream = out_cotangent.astype(F32)
     reduced = [None] * layer_count
-    smalls = [None] * layer_count
     for level in reversed(range(layer_count)):
-        upstream, big, small = layer_backward(
+        upstream, big = layer_backward(
             upstream, weights[level], saved[level], seq_index, seq_size, fsdp_size
         )
-        smalls[level] = small
         reduced[level] = unpack_big(
             reduce_big(big), (hidden_local, D, 3 * D // seq_size, D // seq_size)
         )
-    small_sum = lax.psum(jnp.stack(smalls), ("seq", "fsdp"))
-    vectors = [take_part(small_sum[:, i * D : (i + 1) * D], 1, fsdp_size, owner) for i in range(8)]
-    up_sum = take_part(small_sum[:, 8 * D :], 1, fsdp_size, owner)
-    qkv_grad, out_grad, up_grad, down_grad = [
-        jnp.stack([reduced[level][member] for level in range(layer_count)]) for member in range(4)
+    qkv_grad, out_grad, up_grad, down_grad, small_grad = [
+        jnp.stack([reduced[level][member] for level in range(layer_count)]) for member in range(5)
     ]
+    vectors = [small_grad[:, :, i] for i in range(8)]
+    up_sum = small_grad[:, :, 8:12].reshape(layer_count, -1)
     return (
         frames_out,
         upstream,

time: 1100 us -> 746 us (0.68)
  waiting for transfers between devices: 753 us -> 210 us
  Pallas kernels: 0 us -> 208 us
  local copies, waits for them, and re-layouts: 74.5 us -> 111 us
  blocking collectives: 32.3 us -> 0 us
  other arithmetic: 69.5 us -> 52 us
    reduce_scatter x8 -> x0, waiting for transfers between devices: 219 us -> none  [seq_reduce(): lax.psum_scatter(partial_sum.astype(BF), 'seq', scatter_dimension=1, tile...]
    pallas_call x0 -> x16, Pallas kernels: none -> 208 us  [the longest x8 106 us: seq_reduce(): pl.pallas_call(reduce_kernel, out_shape=jax.ShapeDtypeStruct((rows, width...]
    all_gather x2, waiting for transfers between devices: 157 us -> 29.6 us  [local(): packed = lax.all_gather(packed, 'fsdp', axis=0, tiled=True)]
    psum x1 -> x0, waiting for transfers between devices: 109 us -> none  [local(): small_sum = lax.psum(jnp.stack(smalls), ('seq', 'fsdp'))]
    all_gather x8 -> x2, waiting for transfers between devices: 119 us -> 58.2 us  [local(): lead = lax.all_gather(lead, 'fsdp', axis=0, tiled=True)]
    all_gather x1 -> x0, blocking collectives: 32.3 us -> none  [local(): lax.all_gather(small_in.reshape(-1), 'fsdp', axis=0, tiled=False)]
    another operation x10 -> x47, local copies, waits for them, and re-layouts: 0.34 us -> 26.3 us  [the longest x23 13.7 us: local(): jnp.stack([norm1_gain[level], norm1_bias[level], qv_bias[level, 0], qv_bi...]
    reduce_scatter x2, waiting for transfers between devices: 96.8 us -> 81.2 us  [reduce_big(): owned = lax.psum_scatter(big, 'fsdp', scatter_dimension=0, tiled=True)]
  transfers between devices with their start and end apart: 25 -> 10, of which waited for: 24 -> 6; matrix products, arithmetic and copies ran while one was open for 12% -> 21% of each run, Pallas kernels for 0% -> 20%
where the time goes in v2:
time: 746 us; the launch traced here: 736 us
  waiting for transfers between devices  210 us (28%)
  Pallas kernels  208 us (28%)
  matrix products  130 us (17%)
  local copies, waits for them, and re-layouts  111 us (15%)
  other arithmetic  52 us (7%)
  between operations  16.4 us (2%)
  starting transfers between devices  8.72 us (1%)
    pallas_call x8, Pallas kernels, seq_reduce(): pl.pallas_call(reduce_kernel, out_shape=jax.ShapeDtypeStruct((rows, width...  106 us
    pallas_call x8, Pallas kernels, seq_gather(): pl.pallas_call(gather_kernel, out_shape=jax.ShapeDtypeStruct((4, rows, wi...  102 us
    reduce_scatter x2, waiting for transfers between devices, reduce_big(): owned = lax.psum_scatter(big, 'fsdp', scatter_dimension=0, tiled=True)  81.2 us
    all_gather x2, waiting for transfers between devices, local(): lead = lax.all_gather(lead, 'fsdp', axis=0, tiled=True)  58.2 us
    dot_general x8, matrix products, dot_in(): return jnp.einsum('cfi,io->cfo', rows, matrix, preferred_element_type=F32)  49.8 us
    all_gather x2, waiting for transfers between devices, reduce_big(): return lax.all_gather(owned, 'seq', axis=0, tiled=False)  39.8 us
    all_gather x2, waiting for transfers between devices, local(): packed = lax.all_gather(packed, 'fsdp', axis=0, tiled=True)  29.6 us
    unnamed x205, local copies, waits for them, and re-layouts  21.4 us
  transfers between devices with their start and end apart: 10, of which 6 were waited for; matrix products, arithmetic and copies ran while one was open for 21% of the time, Pallas kernels for 20%

profile of v2, /device:TPU:0, one launch (start us, length us, event | category | flops | bytes accessed | tf_op | source)
XLA Modules:
  0.0 736.0 jit_solution(17119859745634919242)
XLA Ops:
  30.8 14.2 %shard_map.253 = bf16[4,256,768]{2,1,0:T(8,128)(2,1)S(1)} custom-call(bf16[256,768]{1,0:T(8,128)(2,1)S(1)} %bitcast.322), custom_call_target="tpu_custom_call" | custom-call | bytes 3145728 | tf_op jit(solution)/shard_map/pallas_call | solution.py:115
  45.6 18.9 %all-gather.9.cloned.1.call-done = bf16[768,704]{1,0:T(8,128)(2,1)} async-done(((bf16[96,704]{1,0:T(8,128)(2,1)}), bf16[768,704]{1,0:T(8,128)(2,1)}) %all-gather.9.cloned.1.call-update) | async-done | bytes 1081360 | tf_op jit(solution)/shard_map/all_gather | solution.py:390
  67.7 39.4 %all-gather.13.cloned.1.call-done = bf16[768,704]{1,0:T(8,128)(2,1)} async-done(((bf16[96,704]{1,0:T(8,128)(2,1)}), bf16[768,704]{1,0:T(8,128)(2,1)}) %all-gather.13.cloned.1.call-update) | async-done | bytes 1081360 | tf_op jit(solution)/shard_map/all_gather | solution.py:390
  115.8 12.7 %shard_map.245 = bf16[4,256,768]{2,1,0:T(8,128)(2,1)S(1)} custom-call(bf16[256,768]{1,0:T(8,128)(2,1)S(1)} %fusion.86.block_ref), custom_call_target="tpu_custom_call" | custom-call | bytes 3145728 | tf_op jit(solution)/shard_map/pallas_call | solution.py:115
  144.3 29.6 %all-gather.11.cloned.1.call-done = bf16[768,2304]{1,0:T(8,128)(2,1)} async-done(((bf16[96,2304]{1,0:T(8,128)(2,1)}), bf16[768,2304]{1,0:T(8,128)(2,1)}) %all-gather.11.cloned.1.call-update) | async-done | bytes 3538960 | tf_op jit(solution)/shard_map/all_gather | solution.py:399
  176.2 13.2 %shard_map.246 = f32[256,768]{1,0:T(8,128)S(1)} custom-call(bf16[4,256,768]{2,1,0:T(8,128)(2,1)S(1)} %bitcast.316), custom_call_target="tpu_custom_call" | custom-call | bytes 3145728 | tf_op jit(solution)/shard_map/pallas_call | solution.py:137
  190.2 12.5 %shard_map.247 = bf16[4,256,768]{2,1,0:T(8,128)(2,1)S(1)} custom-call(bf16[256,768]{1,0:T(8,128)(2,1)S(1)} %fusion.83.block_ref), custom_call_target="tpu_custom_call" | custom-call | bytes 3145728 | tf_op jit(solution)/shard_map/pallas_call | solution.py:115
  202.7 9.2 %multiply_convert_fusion.3 = (bf16[1024,768]{1,0:T(8,128)(2,1)S(1)}, f32[1024,768]{1,0:T(8,128)}, f32[1024,768]{1,0:T(8,128)}) fusion(f32[768]{0:T(1024)S(1)} %add.274, bf16[1024,768]{1,0:T(8,128)(2,1)S(1)} %bitcast.331, bf16[768,2304]{1,0:T(8,128)(2,1)S(1)} %copy-done.35), kind=kOutput, calls=%fused_computation.49 | convolution fusion | flops 1259864064 | bytes 10620928 | tf_op jit(solution)/shard_map/cfi,io->cfo/dot_general | solution.py:155
  213.4 13.3 %shard_map.248 = f32[256,768]{1,0:T(8,128)S(1)} custom-call(bf16[4,256,768]{2,1,0:T(8,128)(2,1)S(1)} %bitcast.327), custom_call_target="tpu_custom_call" | custom-call | bytes 3145728 | tf_op jit(solution)/shard_map/pallas_call | solution.py:137
  227.4 12.4 %shard_map.249 = bf16[4,256,768]{2,1,0:T(8,128)(2,1)S(1)} custom-call(bf16[256,768]{1,0:T(8,128)(2,1)S(1)} %fusion.84.block_ref), custom_call_target="tpu_custom_call" | custom-call | bytes 3145728 | tf_op jit(solution)/shard_map/pallas_call | solution.py:115
  253.7 13.3 %shard_map.250 = f32[256,768]{1,0:T(8,128)S(1)} custom-call(bf16[4,256,768]{2,1,0:T(8,128)(2,1)S(1)} %bitcast.317), custom_call_target="tpu_custom_call" | custom-call | bytes 3145728 | tf_op jit(solution)/shard_map/pallas_call | solution.py:137
  267.6 12.3 %shard_map.251 = bf16[4,256,768]{2,1,0:T(8,128)(2,1)S(1)} custom-call(bf16[256,768]{1,0:T(8,128)(2,1)S(1)} %fusion.85.block_ref), custom_call_target="tpu_custom_call" | custom-call | bytes 3145728 | tf_op jit(solution)/shard_map/pallas_call | solution.py:115
  279.9 31.5 %multiply_convert_fusion.2 = (bf16[1024,768]{1,0:T(8,128)(2,1)S(1)}, f32[1024,768]{1,0:T(8,128)S(1)}, f32[1024,768]{1,0:T(8,128)S(1)}) fusion(f32[768]{0:T(1024)S(1)} %copy-done.85, bf16[1024,768]{1,0:T(8,128)(2,1)S(1)} %bitcast.339, bf16[768,2304]{1,0:T(8,128)(2,1)S(1)} %copy-done.36), kind=kOutput, calls=%fused_computation.36 | convolution fusion | flops 1259864064 | bytes 10620928 | tf_op jit(solution)/shard_map/cfi,io->cfo/dot_general | solution.py:155
  312.9 13.3 %shard_map.252 = f32[256,768]{1,0:T(8,128)S(1)} custom-call(bf16[4,256,768]{2,1,0:T(8,128)(2,1)S(1)} %bitcast.328), custom_call_target="tpu_custom_call" | custom-call | bytes 3145728 | tf_op jit(solution)/shard_map/pallas_call | solution.py:137
  333.1 12.6 %shard_map.254 = f32[256,768]{1,0:T(8,128)S(1)} custom-call(bf16[4,256,768]{2,1,0:T(8,128)(2,1)S(1)} %bitcast.323), custom_call_target="tpu_custom_call" | custom-call | bytes 3145728 | tf_op jit(solution)/shard_map/pallas_call | solution.py:137
  348.6 12.6 %shard_map.255 = bf16[4,256,768]{2,1,0:T(8,128)(2,1)S(1)} custom-call(bf16[256,768]{1,0:T(8,128)(2,1)S(1)} %bitcast.341), custom_call_target="tpu_custom_call" | custom-call | bytes 3145728 | tf_op jit(solution)/shard_map/pallas_call | solution.py:115
  408.9 13.3 %shard_map.256 = f32[256,768]{1,0:T(8,128)S(1)} custom-call(bf16[4,256,768]{2,1,0:T(8,128)(2,1)S(1)} %bitcast.324), custom_call_target="tpu_custom_call" | custom-call | bytes 3145728 | tf_op jit(solution)/shard_map/pallas_call | solution.py:137
  428.7 13.1 %shard_map.257 = bf16[4,256,768]{2,1,0:T(8,128)(2,1)S(1)} custom-call(bf16[256,768]{1,0:T(8,128)(2,1)S(1)} %convert_bitcast_fusion.1.block_ref), custom_call_target="tpu_custom_call" | custom-call | bytes 3145728 | tf_op jit(solution)/shard_map/pallas_call | solution.py:115
  451.0 13.3 %shard_map.258 = f32[256,768]{1,0:T(8,128)S(1)} custom-call(bf16[4,256,768]{2,1,0:T(8,128)(2,1)S(1)} %bitcast.325), custom_call_target="tpu_custom_call" | custom-call | bytes 3145728 | tf_op jit(solution)/shard_map/pallas_call | solution.py:137
  478.5 12.7 %shard_map.259 = bf16[4,256,768]{2,1,0:T(8,128)(2,1)S(1)} custom-call(bf16[256,768]{1,0:T(8,128)(2,1)S(1)} %convert_bitcast_fusion.block_ref), custom_call_target="tpu_custom_call" | custom-call | bytes 3145728 | tf_op jit(solution)/shard_map/pallas_call | solution.py:115
  527.7 13.3 %shard_map.260 = f32[256,768]{1,0:T(8,128)S(1)} custom-call(bf16[4,256,768]{2,1,0:T(8,128)(2,1)S(1)} %bitcast.326), custom_call_target="tpu_custom_call" | custom-call | bytes 3145728 | tf_op jit(solution)/shard_map/pallas_call | solution.py:137
  571.6 81.2 %reduce-scatter.7.cloned.1.call-done = bf16[96,2432]{1,0:T(8,128)(2,1)} async-done(((bf16[768,2432]{1,0:T(8,128)(2,1)}), bf16[96,2432]{1,0:T(8,128)(2,1)}) %reduce-scatter.7.cloned.1.call-update) | async-done | bytes 466960 | tf_op jit(solution)/shard_map/reduce_scatter | solution.py:259
  653.9 21.3 %all-gather.19.cloned.1.call-done = bf16[384,2432]{1,0:T(8,128)(2,1)} async-done(((bf16[96,2432]{1,0:T(8,128)(2,1)}), bf16[384,2432]{1,0:T(8,128)(2,1)}) %all-gather.19.cloned.1.call-update) | async-done | bytes 1867792 | tf_op jit(solution)/shard_map/all_gather | solution.py:260
  679.7 18.5 %all-gather.17.cloned.1.call-done = bf16[384,2432]{1,0:T(8,128)(2,1)} async-done(((bf16[96,2432]{1,0:T(8,128)(2,1)}), bf16[384,2432]{1,0:T(8,128)(2,1)}) %all-gather.17.cloned.1.call-update) | async-done | bytes 1867792 | tf_op jit(solution)/shard_map/all_gather | solution.py:260
  (464 shorter events, 262.0 us)
Async XLA Ops:
  7.2 57.3 %all-gather.9.cloned.1.call-start = ((), (), s32[]{:S(2)}) async-start(), calls=%async_computation.4 | async-start | bytes 1327104 | tf_op jit(solution)/shard_map/all_gather | solution.py:390
  20.6 86.5 %all-gather.13.cloned.1.call-start = ((), (), s32[]{:S(2)}) async-start(), calls=%async_computation.6 | async-start | bytes 1327104 | tf_op jit(solution)/shard_map/all_gather | solution.py:390
  25.9 147.9 %all-gather.11.cloned.1.call-start = ((), (), s32[]{:S(2)}) async-start(), calls=%async_computation.5 | async-start | bytes 3981312 | tf_op jit(solution)/shard_map/all_gather | solution.py:399
  28.5 222.1 %all-gather.15.cloned.1.call-start = ((), (), s32[]{:S(2)}) async-start(), calls=%async_computation.7 | async-start | bytes 3981312 | tf_op jit(solution)/shard_map/all_gather | solution.py:399
  30.0 84.8 %copy-start.45 = (f32[256]{0:T(256)}, f32[256]{0:T(256)S(1)}, u32[]{:S(2)}) copy-start(f32[256]{0:T(256)S(1)} %broadcast_multiply_fusion.3) | copy-start | bytes 3076
  30.3 37.4 %copy-start.71 = (f32[256]{0:T(256)}, f32[256]{0:T(256)S(1)}, u32[]{:S(2)}) copy-start(f32[256]{0:T(256)S(1)} %fusion.73) | copy-start | bytes 3076
  67.5 48.2 %copy-start.37 = (f32[768]{0:T(1024)}, f32[768]{0:T(1024)S(1)}, u32[]{:S(2)}) copy-start(f32[768]{0:T(1024)S(1)} %get-tuple-element.135) | copy-start | bytes 9220
  67.5 122.4 %copy-start.40 = (f32[768]{0:T(1024)}, f32[768]{0:T(1024)S(1)}, u32[]{:S(2)}) copy-start(f32[768]{0:T(1024)S(1)} %get-tuple-element.130) | copy-start | bytes 9220
  110.1 117.1 %copy-start.42 = (f32[768]{0:T(1024)}, f32[768]{0:T(1024)S(1)}, u32[]{:S(2)}) copy-start(f32[768]{0:T(1024)S(1)} %get-tuple-element.127) | copy-start | bytes 9220
  140.8 48.7 %copy-start.27 = (bf16[3,64,1024]{2,1,0:T(8,128)(2,1)}, bf16[3,64,1024]{2,1,0:T(8,128)(2,1)S(1)}, u32[]{:S(2)}) copy-start(bf16[3,64,1024]{2,1,0:T(8,128)(2,1)S(1)} %fusion.46) | copy-start | bytes 1179652
  143.4 59.4 %copy-start.83 = (f32[768]{0:T(1024)}, f32[768]{0:T(1024)S(1)}, u32[]{:S(2)}) copy-start(f32[768]{0:T(1024)S(1)} %add.274) | copy-start | bytes 9220
  144.3 45.2 %copy-start.60 = (f32[768]{0:T(1024)S(1)}, f32[768]{0:T(1024)}, u32[]{:S(2)}) copy-start(f32[768]{0:T(1024)} %get-tuple-element.131) | copy-start | bytes 9220
  226.9 40.0 %copy-start.13 = (f32[1,256,768]{2,1,0:T(8,128)}, f32[1,256,768]{2,1,0:T(8,128)S(1)}, u32[]{:S(2)}) copy-start(f32[1,256,768]{2,1,0:T(8,128)S(1)} %get-tuple-element.167) | copy-start | bytes 2359300
  331.6 31.4 %slice-start.3 = ((s8[12582912]{0:T(1024)(128)(4,1)}), s8[4194304]{0:T(1024)(128)(4,1)S(1)}, s32[]{:S(2)}) async-start(s8[12582912]{0:T(1024)(128)(4,1)} %bitcast.344), calls=%async_computation.15 | async-start | bytes 8388608
  331.6 31.4 %slice-start.4 = ((s8[12582912]{0:T(1024)(128)(4,1)}), s8[4194304]{0:T(1024)(128)(4,1)S(1)}, s32[]{:S(2)}) async-start(s8[12582912]{0:T(1024)(128)(4,1)} %bitcast.344), calls=%async_computation.16 | async-start | bytes 8388608
  396.4 70.3 %all-to-all-start.1 = ((bf16[192,4,192]{0,2,1:T(8,128)(2,1)}), bf16[192,4,192]{0,2,1:T(8,128)(2,1)}, u32[]{:S(2)}, u32[]{:S(2)}) async-start(bf16[192,4,192]{0,2,1:T(8,128)(2,1)} %bitcast.374), calls=%async_computation.1 | async-start | bytes 786432 | tf_op jit(solution)/shard_map/all_to_all | solution.py:232
  400.5 170.3 %reduce-scatter.9.cloned.1.call-start = ((), (), s32[]{:S(2)}) async-start(), calls=%async_computation.11 | async-start | bytes 4202496 | tf_op jit(solution)/shard_map/reduce_scatter | solution.py:259
  495.4 66.1 %all-to-all-start = ((bf16[192,4,192]{0,2,1:T(8,128)(2,1)}), bf16[192,4,192]{0,2,1:T(8,128)(2,1)}, u32[]{:S(2)}, u32[]{:S(2)}) async-start(bf16[192,4,192]{0,2,1:T(8,128)(2,1)} %bitcast.375), calls=%async_computation | async-start | bytes 786432 | tf_op jit(solution)/shard_map/all_to_all | solution.py:232
  499.5 153.2 %reduce-scatter.7.cloned.1.call-start = ((), (), s32[]{:S(2)}) async-start(), calls=%async_computation.10 | async-start | bytes 4202496 | tf_op jit(solution)/shard_map/reduce_scatter | solution.py:259
  527.7 25.1 %copy-start.4 = (bf16[4,256,768]{2,1,0:T(8,128)(2,1)S(1)}, bf16[4,256,768]{2,1,0:T(8,128)(2,1)}, u32[]{:S(2)}) copy-start(bf16[4,256,768]{2,1,0:T(8,128)(2,1)} %copy-done.3) | copy-start | bytes 4718596
  570.7 82.0 %copy-start.86 = (f32[256]{0:T(256)S(1)}, f32[256]{0:T(256)}, u32[]{:S(2)}) copy-start(f32[256]{0:T(256)} %get-tuple-element.119) | copy-start | bytes 3076
  570.7 82.0 %copy-start.76 = (f32[256]{0:T(256)S(1)}, f32[256]{0:T(256)}, u32[]{:S(2)}) copy-start(f32[256]{0:T(256)} %copy-done.75) | copy-start | bytes 3076
  570.8 104.5 %all-gather.19.cloned.1.call-start = ((), (), s32[]{:S(2)}) async-start(), calls=%async_computation.9 | async-start | bytes 2334720 | tf_op jit(solution)/shard_map/all_gather | solution.py:260
  571.5 126.7 %all-gather.17.cloned.1.call-start = ((), (), s32[]{:S(2)}) async-start(), calls=%async_computation.8 | async-start | bytes 2334720 | tf_op jit(solution)/shard_map/all_gather | solution.py:260
  (85 other events, 861.7 us)
Sparse Core Ops, SparseCore 0:
  20.7 43.7 all-gather.8
  67.2 39.8 all-gather.12
  109.8 63.9 all-gather.10
  176.5 63.6 all-gather.14
  475.9 80.8 reduce-scatter.8
  570.9 81.7 reduce-scatter.6
  654.3 20.9 all-gather.18
  676.9 21.2 all-gather.16
